TPU v7x, 32 devices: a whole 2x2x4 slice. The times are simulated.
32 devices in a mesh: lat: 4 (over x, core), lon: 8 (over z, y).
Axes of the slice: x: 2, y: 2, z: 4, core: 2. Of those that a mesh axis runs over, the one named last changes fastest.
Arguments:
- tracers: float32 [4, 32, 128, 1024], P(None, None, 'lat', 'lon'), may hold values from -6 to 6
- vel_east: float32 [32, 128, 1024], P(None, 'lat', 'lon'), may hold values from -0.18 to 0.18
- vel_north: float32 [32, 128, 1024], P(None, 'lat', 'lon'), may hold values from -0.18 to 0.18
- land_mask: int32 [32, 128, 1024], P(None, 'lat', 'lon'), may hold values 0 or 1
- step_area: float32 [128, 1024], P('lat', 'lon'), may hold values from 1.5 to 4
- float_cell: int32 [2048], P(('lat', 'lon')), may hold values from 0 to 4095
- float_owner: int32 [2048, 1], P(('lat', 'lon')), may hold values from 0 to 31; in each aligned block of 64 rows (0 to 63, 64 to 127, ...) at most 4 rows name the same one
Outputs:
- tracers_out: float32 [4, 32, 128, 1024], P(None, None, 'lat', 'lon')
- arrivals: float32 [4096, 128], P(('lat', 'lon'))
- arrival_counts: int32 [1024], P(('lat', 'lon'))
Inputs may be any that keep to these rules, and one draw needn't show every extreme that they name: `float_owner`: among the 64 rows of one device no device number appears more than 4 times, and in some device's rows one appears exactly 4 times.
All inputs are finite; a program needn't handle non-finite values. No bound on the sum of `land_mask` on one device may be relied on, other than what follows from the above.
Results may differ from a plain program's by a relative error of at most 0.0003.
Values sent between devices are 32-bit elements; how exact they have to be, the bound alone decides.
A program may use at most 128 MiB of HBM per device.

v0:
```python
import jax
import jax.numpy as jnp
from jax import lax
from jax.sharding import PartitionSpec as P

CAP = 4


def partner(shard, axis, stride):
    return lax.ppermute(shard, axis, [(i, i ^ 1 << stride) for i in range(lax.axis_size(axis))])


def padded(block, sides, width, periodic):
    for axis, dim in sides:
        count = lax.axis_size(axis)
        forward = [(i, i + 1) for i in range(count - 1)]
        if periodic:
            forward.append((count - 1, 0))
        backward = [(target, source) for source, target in forward]
        low = lax.ppermute(
            lax.slice_in_dim(block, block.shape[dim] - width, None, axis=dim), axis, forward
        )
        high = lax.ppermute(lax.slice_in_dim(block, 0, width, axis=dim), axis, backward)
        block = jnp.concatenate([low, block, high], axis=dim)
    return block


def face_flux(velocity, behind, current, forward, farther):
    return (
        velocity * (7.0 * (current + forward) - (behind + farther)) / 12.0
        - jnp.abs(velocity) * (3.0 * (forward - current) - (farther - behind)) / 12.0
    )


def advance(tracer_pad, static_pad, step_area):
    row_count = tracer_pad.shape[-2] - 4
    col_count = tracer_pad.shape[-1] - 4
    flow_east, flow_north, wet_pad = (static_pad[0], static_pad[1], static_pad[2])
    lon_strip = tracer_pad[..., 2 : row_count + 2, :]
    open_east = (
        flow_east[:, 2 : row_count + 2, 1 : col_count + 2]
        * wet_pad[:, 2 : row_count + 2, 1 : col_count + 2]
        * wet_pad[:, 2 : row_count + 2, 2 : col_count + 3]
    )
    flux_x = face_flux(
        open_east,
        lon_strip[..., 0 : col_count + 1],
        lon_strip[..., 1 : col_count + 2],
        lon_strip[..., 2 : col_count + 3],
        lon_strip[..., 3 : col_count + 4],
    )
    lat_strip = tracer_pad[..., 2 : col_count + 2]
    open_north = (
        flow_north[:, 1 : row_count + 2, 2 : col_count + 2]
        * wet_pad[:, 1 : row_count + 2, 2 : col_count + 2]
        * wet_pad[:, 2 : row_count + 3, 2 : col_count + 2]
    )
    flux_y = face_flux(
        open_north,
        lat_strip[..., 0 : row_count + 1, :],
        lat_strip[..., 1 : row_count + 2, :],
        lat_strip[..., 2 : row_count + 3, :],
        lat_strip[..., 3 : row_count + 4, :],
    )
    change = flux_x[..., 1:] - flux_x[..., :-1] + (flux_y[..., 1:, :] - flux_y[..., :-1, :])
    centre = tracer_pad[..., 2 : row_count + 2, 2 : col_count + 2]
    return centre - step_area * wet_pad[:, 2 : row_count + 2, 2 : col_count + 2] * change


def local(tracers, vel_east, vel_north, land_mask, step_area, float_cell, float_owner):
    tracer_count = tracers.shape[0]
    level_count = tracers.shape[1]
    row_count = tracers.shape[2]
    col_count = tracers.shape[3]
    at_top = lax.axis_index("lat") == lax.axis_size("lat") - 1
    wet_mask = land_mask.astype(jnp.float32)
    bit_count = lax.axis_size("lon").bit_length() - 1

    def mirror(payload):
        moving = jnp.flip(payload, axis=(2, 3))
        for bit_number in range(bit_count):
            moving = partner(moving, "lon", bit_number)
        return moving

    def add_rims(field_in, ghost_rows):
        lat_padded = padded(field_in, (("lat", 2),), 2, False)
        upper_rows = jnp.where(at_top, ghost_rows, lat_padded[:, :, row_count + 2 :, :])
        lat_padded = jnp.concatenate([lat_padded[:, :, : row_count + 2, :], upper_rows], axis=2)
        return padded(lat_padded, (("lon", 3),), 2, True)

    mirrored = mirror(
        jnp.concatenate(
            [tracers[:, :, row_count - 2 :, :], wet_mask[None, :, row_count - 2 :, :]], axis=0
        )
    )
    joined = jnp.concatenate([tracers, vel_east[None], vel_north[None], wet_mask[None]], axis=0)
    still_rows = jnp.zeros((2, level_count, 2, col_count), jnp.float32)
    ghost_rows = jnp.concatenate(
        [mirrored[:tracer_count], still_rows, mirrored[tracer_count:]], axis=0
    )
    full_padded = add_rims(joined, ghost_rows)
    tracer_pad = full_padded[:tracer_count]
    static_pad = full_padded[tracer_count:]
    after_one = advance(tracer_pad, static_pad, step_area)
    second = advance(
        add_rims(after_one, mirror(after_one[:, :, row_count - 2 :, :])), static_pad, step_area
    )
    flat_values = second.reshape(tracer_count * level_count, row_count * col_count)
    records = jnp.take(flat_values, float_cell, axis=1).T
    owner = float_owner[:, 0]
    float_count = owner.shape[0]
    devices_all = lax.axis_size("lat") * lax.axis_size("lon")
    local_index = jnp.arange(float_count, dtype=jnp.int32)
    same_owner = (owner[:, None] == owner[None, :]) & (local_index[None, :] < local_index[:, None])
    slot_rank = jnp.sum(same_owner.astype(jnp.int32), axis=1)
    slot_index = owner * CAP + slot_rank
    outbox = (
        jnp.zeros((devices_all * CAP, records.shape[1]), jnp.float32).at[slot_index].set(records)
    )
    sent_count = jnp.sum(
        (jnp.arange(devices_all, dtype=jnp.int32)[:, None] == owner[None, :]).astype(jnp.float32),
        axis=1,
    )
    received, arrived_count = (
        lax.all_to_all(outbox, ("lat", "lon"), split_axis=0, concat_axis=0, tiled=True),
        lax.all_to_all(
            sent_count[:, None], ("lat", "lon"), split_axis=0, concat_axis=0, tiled=True
        ),
    )
    return (second, received, arrived_count.reshape(devices_all).astype(jnp.int32))


def solution(mesh):
    placed = (
        P(None, None, "lat", "lon"),
        P(None, "lat", "lon"),
        P(None, "lat", "lon"),
        P(None, "lat", "lon"),
        P("lat", "lon"),
        P(("lat", "lon")),
        P(("lat", "lon"), None),
    )
    return jax.shard_map(
        local,
        mesh=mesh,
        in_specs=placed,
        out_specs=(P(None, None, "lat", "lon"), P(("lat", "lon"), None), P(("lat", "lon"))),
        check_vma=False,
    )
```

profile of v0, /device:TPU:0, one launch (start us, length us, event | category | flops | bytes accessed | tf_op | source)
XLA Modules:
  0.0 169.1 jit_solution(14256752070223755826)
XLA Ops:
  0.6 2.9 %copy.63 = f32[4,32,32,128]{3,1,2,0:T(8,128)S(1)} copy(f32[4,32,32,128]{3,2,1,0:T(8,128)} %param.7) | data formatting | bytes 4194304 | tf_op args[0]
  3.5 0.3 copy_convert_fusion
  4.0 3.0 %collective-permute-start.1 = (f32[5,32,2,128]{3,1,2,0:T(8,128)S(1)}, f32[5,32,2,128]{3,1,2,0:T(8,128)S(1)}, u32[]{:S(2)}, u32[]{:S(2)}) collective-permute-start(f32[5,32,2,128]{3,1,2,0:T(8,128)S(1)} %rev.8), channel_id=1, source_target_pairs={{0,1},{1,0},{2,3},{3,2},{4,5},{5,4},{6,7},{7,6},{8,9},{9,8},{10,11... | collective-permute-start | bytes 491528 | tf_op jit(solution)/shard_map/ppermute | solution.py:10
  7.0 4.2 %collective-permute-done.1 = f32[5,32,2,128]{3,1,2,0:T(8,128)S(1)} collective-permute-done((f32[5,32,2,128]{3,1,2,0:T(8,128)S(1)}, f32[5,32,2,128]{3,1,2,0:T(8,128)S(1)}, u32[]{:S(2)}, u32[]{:S(2)}) %collective-permute-start.1) | collective-permute-done | bytes 163872 | tf_op jit(solution)/shard_map/ppermute | solution.py:10
  11.2 1.8 %collective-permute-start.2 = (f32[5,32,2,128]{3,1,2,0:T(8,128)S(1)}, f32[5,32,2,128]{3,1,2,0:T(8,128)}, u32[]{:S(2)}, u32[]{:S(2)}) collective-permute-start(f32[5,32,2,128]{3,1,2,0:T(8,128)S(1)} %collective-permute-done.1), channel_id=1, source_target_pairs={{0,2},{1,3},{2,0},{3,1},{4,6},{5,7},{6,4},{7,5},{8,10},{9,11},{10,... | collective-permute-start | bytes 491528 | tf_op jit(solution)/shard_map/ppermute | solution.py:10
  13.0 1.8 %copy_bitcast_fusion.1 = (f32[1,32,32,128]{3,1,2,0:T(8,128)S(1)}, f32[1,32,32,128]{3,1,2,0:T(8,128)S(1)}) fusion(f32[32,32,128]{2,1,0:T(8,128)} %param.9, f32[32,32,128]{2,1,0:T(8,128)} %param.8), kind=kLoop, calls=%fused_computation.43 | loop fusion | bytes 2097152 | tf_op jit(solution)/shard_map/broadcast_in_dim | solution.py:96
  14.9 0.8 copy-done.2
  15.6 0.7 pad_maximum_fusion.11
  16.4 1.3 collective-permute-start.4
  17.7 3.7 %collective-permute-start = (f32[7,32,2,128]{3,1,2,0:T(8,128)}, f32[7,32,2,128]{3,1,2,0:T(8,128)}, u32[]{:S(2)}, u32[]{:S(2)}) collective-permute-start(f32[7,32,2,128]{3,1,2,0:T(8,128)} %get-tuple-element.25), channel_id=1, source_target_pairs={{0,8},{8,16},{16,24},{1,9},{9,17},{17,25},{2,10},{10,18},{18,26},{... | collective-permute-start | bytes 688136 | tf_op jit(solution)/shard_map/ppermute | solution.py:20
  21.4 2.6 %collective-permute-start.3 = (f32[5,32,2,128]{3,1,2,0:T(8,128)}, f32[5,32,2,128]{3,1,2,0:T(8,128)S(1)}, u32[]{:S(2)}, u32[]{:S(2)}) collective-permute-start(f32[5,32,2,128]{3,1,2,0:T(8,128)} %collective-permute-done.2), channel_id=1, source_target_pairs={{0,4},{1,5},{2,6},{3,7},{4,0},{5,1},{6,2},{7,3},{8,12},{9,13},{10,... | collective-permute-start | bytes 491528 | tf_op jit(solution)/shard_map/ppermute | solution.py:10
  24.0 0.1 convert_reduce_fusion.2
  24.1 0.7 copy.70
  24.8 2.9 %all-to-all-start.1 = ((f32[32,1,1]{2,1,0:T(1,128)}), f32[32,1,1]{2,1,0:T(1,128)S(1)}, u32[]{:S(2)}, u32[]{:S(2)}) async-start(f32[32,1,1]{2,1,0:T(1,128)} %copy.70), calls=%async_computation.1 | async-start | bytes 32768 | tf_op jit(solution)/shard_map/all_to_all | solution.py:126
  27.8 1.4 convert_reduce_fusion
  29.2 3.4 %collective-permute-done.3 = f32[5,32,2,128]{3,1,2,0:T(8,128)S(1)} collective-permute-done((f32[5,32,2,128]{3,1,2,0:T(8,128)}, f32[5,32,2,128]{3,1,2,0:T(8,128)S(1)}, u32[]{:S(2)}, u32[]{:S(2)}) %collective-permute-start.3) | collective-permute-done | bytes 163872 | tf_op jit(solution)/shard_map/ppermute | solution.py:10
  32.7 1.0 maximum_select_fusion
  33.7 1.5 pad_maximum_fusion.3
  35.3 4.7 %fusion.19 = (f32[7,32,36,2]{3,1,2,0:T(8,128)}, f32[7,32,36,2]{3,1,2,0:T(8,128)}) fusion(f32[7,32,36,128]{3,1,2,0:T(8,128)S(1)} %pad_maximum_fusion.3), kind=kLoop, calls=%fused_computation.74 | loop fusion | bytes 258048 | tf_op jit(solution)/shard_map/slice | solution.py:21
  40.0 4.2 %copy.57 = f32[7,32,36,2]{2,1,3,0:T(8,128)} copy(f32[7,32,36,2]{3,1,2,0:T(8,128)} %get-tuple-element.21) | data formatting | bytes 129024 | tf_op jit(solution)/shard_map/slice | solution.py:21
  44.2 1.5 collective-permute-start.5
  45.7 4.2 %copy.58 = f32[7,32,36,2]{2,1,3,0:T(8,128)} copy(f32[7,32,36,2]{3,1,2,0:T(8,128)} %get-tuple-element.22) | data formatting | bytes 129024 | tf_op jit(solution)/shard_map/slice | solution.py:23
  49.9 3.2 %collective-permute-start.6 = (f32[7,32,36,2]{2,1,3,0:T(8,128)}, f32[7,32,36,2]{2,1,3,0:T(8,128)}, u32[]{:S(2)}, u32[]{:S(2)}) collective-permute-start(f32[7,32,36,2]{2,1,3,0:T(8,128)} %copy.58), channel_id=1, source_target_pairs={{1,0},{2,1},{3,2},{4,3},{5,4},{6,5},{7,6},{0,7},{9,8},{10,9},{11,1... | collective-permute-start | bytes 193544 | tf_op jit(solution)/shard_map/ppermute | solution.py:23
  53.1 4.7 %maximum_maximum_fusion.2 = (f32[7,32,34,128]{3,1,2,0:T(8,128)}, f32[7,32,34,128]{3,1,2,0:T(8,128)}) fusion(f32[1,32,32,128]{3,1,2,0:T(8,128)S(1)} %get-tuple-element.34, f32[1,32,32,128]{3,1,2,0:T(8,128)S(1)} %get-tuple-element.35, f32[1,32,32,128]{3,1,2,0:T(8,128)} %copy-done.2, f32[4,32,32,128]{3,1,2,0:T(8,128)S(1)} %copy.63, ...), kind=kLoop, calls=%fused_computation.10 | loop fusion | flops 7798784 | bytes 11927552 | tf_op jit(solution)/shard_map/concatenate | solution.py:88
  57.9 4.2 %copy.59 = f32[7,32,36,2]{3,1,2,0:T(8,128)} copy(f32[7,32,36,2]{2,1,3,0:T(8,128)} %collective-permute-done.5) | data formatting | bytes 129024 | tf_op jit(solution)/shard_map/ppermute | solution.py:20
  62.0 4.3 %copy.60 = f32[7,32,36,2]{3,1,2,0:T(8,128)} copy(f32[7,32,36,2]{2,1,3,0:T(8,128)} %collective-permute-done.6) | data formatting | bytes 129024 | tf_op jit(solution)/shard_map/ppermute | solution.py:23
  66.3 11.6 %pad_maximum_fusion = f32[7,32,36,132]{3,1,2,0:T(8,128)S(1)} fusion(f32[7,32,36,2]{3,1,2,0:T(8,128)} %copy.60, f32[7,32,2,128]{3,1,2,0:T(8,128)S(1)} %maximum_select_fusion, f32[1,32,32,128]{3,1,2,0:T(8,128)S(1)} %get-tuple-element.34, f32[1,32,32,128]{3,1,2,0:T(8,128)S(1)} %get-tuple-element.35, f32[1,32,32,128]{3,1,2,0:T(8,128)} %copy-done.2, ...), kind=kLoop, calls=%fused_computation.2 | loop fusion | flops 7451136 | bytes 8515584 | tf_op jit(solution)/shard_map/concatenate | solution.py:24
  77.9 0.3 slice_bitcast_fusion.1
  78.2 2.2 %fusion.17 = (f32[32,32,129]{2,0,1:T(8,128)}, f32[32,32,129]{2,0,1:T(8,128)}) fusion(f32[32,36,132]{2,0,1:T(8,128)S(1)} %get-tuple-element.18, f32[32,36,132]{2,0,1:T(8,128)S(1)} %get-tuple-element.16), kind=kLoop, calls=%fused_computation.72 | loop fusion | flops 396288 | bytes 2641920 | tf_op jit(solution)/shard_map/abs | solution.py:31
  80.4 1.5 fusion.18
  82.0 1.0 slice_multiply_fusion.4
  83.0 9.6 %maximum_maximum_fusion = (f32[7,32,36,130]{3,1,2,0:T(8,128)S(1)}, f32[7,32,36,130]{3,1,2,0:T(8,128)S(1)}) fusion(f32[7,32,2,128]{3,1,2,0:T(8,128)S(1)} %maximum_select_fusion, f32[1,32,32,128]{3,1,2,0:T(8,128)S(1)} %get-tuple-element.34, f32[1,32,32,128]{3,1,2,0:T(8,128)S(1)} %get-tuple-element.35, f32[1,32,32,128]{3,1,2,0:T(8,128)S(1)} %copy-done.3, ...), kind=kLoop, calls=%fused_computation.3 | loop fusion | flops 12579840 | bytes 12644352 | tf_op jit(solution)/shard_map/concatenate | solution.py:24
  92.7 4.1 %multiply_subtract_fusion.1 = f32[4,32,32,129]{3,1,2,0:T(8,128)S(1)} fusion(f32[7,32,36,130]{3,1,2,0:T(8,128)S(1)} %get-tuple-element.20, f32[7,32,36,130]{3,1,2,0:T(8,128)S(1)} %get-tuple-element.19, f32[32,32,129]{2,0,1:T(8,128)} %get-tuple-element.12, f32[32,32,129]{2,0,1:T(8,128)} %get-tuple-element.13), kind=kLoop, calls=%fused_computation.8 | loop fusion | flops 6868992 | bytes 11624448 | tf_op jit(solution)/shard_map/sub | solution.py:30
  96.8 0.9 multiply_subtract_fusion.3
  97.7 0.7 copy-done.9
  98.5 2.0 %fusion.7 = f32[4,32,32,128]{3,1,2,0:T(8,128)S(1)} fusion(f32[4,32,33,128]{3,1,2,0:T(8,128)S(1)} %multiply_subtract_fusion.3, f32[4,32,32,129]{3,1,2,0:T(8,128)S(1)} %multiply_subtract_fusion.1, f32[32,32,128]{2,0,1:T(8,128)S(1)} %copy-done.13, f32[4,32,32,128]{3,2,1,0:T(8,128)S(1)} %copy-done.9), kind=kLoop, calls=%fused_computation.32 | loop fusion | flops 2621440 | bytes 13107200 | tf_op jit(solution)/shard_map/sub | solution.py:67
  100.7 0.5 fusion.14
  101.2 4.4 %collective-permute-done.8 = f32[4,32,2,128]{3,1,2,0:T(8,128)S(1)} collective-permute-done((f32[4,32,2,128]{3,1,2,0:T(8,128)S(1)}, f32[4,32,2,128]{3,1,2,0:T(8,128)S(1)}, u32[]{:S(2)}, u32[]{:S(2)}) %collective-permute-start.8) | collective-permute-done | bytes 131104 | tf_op jit(solution)/shard_map/ppermute | solution.py:10
  105.7 1.3 collective-permute-start.11
  107.0 3.7 %collective-permute-done.9 = f32[4,32,2,128]{3,1,2,0:T(8,128)S(1)} collective-permute-done((f32[4,32,2,128]{3,1,2,0:T(8,128)S(1)}, f32[4,32,2,128]{3,1,2,0:T(8,128)S(1)}, u32[]{:S(2)}, u32[]{:S(2)}) %collective-permute-start.9) | collective-permute-done | bytes 131104 | tf_op jit(solution)/shard_map/ppermute | solution.py:10
  110.6 0.5 compare_and_fusion
  111.1 0.6 pad_clamp_fusion
  111.7 1.3 collective-permute-start.7
  113.0 4.3 %collective-permute-done.10 = f32[4,32,2,128]{3,1,2,0:T(8,128)S(1)} collective-permute-done((f32[4,32,2,128]{3,1,2,0:T(8,128)S(1)}, f32[4,32,2,128]{3,1,2,0:T(8,128)S(1)}, u32[]{:S(2)}, u32[]{:S(2)}) %collective-permute-start.10) | collective-permute-done | bytes 131104 | tf_op jit(solution)/shard_map/ppermute | solution.py:10
  117.4 0.2 pad_maximum_fusion.5
  117.6 3.0 %fusion.20 = (f32[4,32,36,2]{3,1,2,0:T(8,128)}, f32[4,32,36,2]{3,1,2,0:T(8,128)}) fusion(f32[4,32,36,128]{3,1,2,0:T(8,128)S(1)} %pad_maximum_fusion.5), kind=kLoop, calls=%fused_computation.75 | loop fusion | bytes 147456 | tf_op jit(solution)/shard_map/slice | solution.py:21
  120.6 3.0 %copy.64 = f32[4,32,36,2]{2,1,3,0:T(8,128)S(1)} copy(f32[4,32,36,2]{3,1,2,0:T(8,128)} %get-tuple-element.29) | data formatting | bytes 73728 | tf_op jit(solution)/shard_map/slice | solution.py:21
  123.6 0.2 collective-permute-start.12
  123.8 3.0 %copy.66 = f32[4,32,36,2]{2,1,3,0:T(8,128)S(1)} copy(f32[4,32,36,2]{3,1,2,0:T(8,128)} %get-tuple-element.30) | data formatting | bytes 73728 | tf_op jit(solution)/shard_map/slice | solution.py:23
  126.7 4.6 %collective-permute-start.13 = (f32[4,32,36,2]{2,1,3,0:T(8,128)S(1)}, f32[4,32,36,2]{2,1,3,0:T(8,128)S(1)}, u32[]{:S(2)}, u32[]{:S(2)}) collective-permute-start(f32[4,32,36,2]{2,1,3,0:T(8,128)S(1)} %copy.66), channel_id=1, source_target_pairs={{1,0},{2,1},{3,2},{4,3},{5,4},{6,5},{7,6},{0,7},{9,8},{10,9},{11,1... | collective-permute-start | bytes 110600 | tf_op jit(solution)/shard_map/ppermute | solution.py:23
  131.3 3.4 %multiply_subtract_fusion.2 = f32[4,32,33,128]{3,1,2,0:T(8,128)} fusion(f32[4,32,32,128]{3,1,2,0:T(8,128)S(1)} %fusion.7, f32[4,32,2,128]{3,1,2,0:T(8,128)S(1)} %collective-permute-done.7, f32[4,32,2,128]{3,1,2,0:T(8,128)S(1)} %broadcast_select_fusion, f32[32,33,128]{2,0,1:T(8,128)S(1)} %copy-done.11, f32[32,33,128]{2,0,1:T(8,128)} %get-tuple-element.15), kind=kLoop, calls=%fused_computation.21 | loop fusion | flops 9191424 | bytes 5603328 | tf_op jit(solution)/shard_map/sub | solution.py:30
  134.7 3.3 %copy.65 = f32[4,32,36,2]{3,1,2,0:T(8,128)} copy(f32[4,32,36,2]{2,1,3,0:T(8,128)S(1)} %collective-permute-done.12) | data formatting | bytes 73728 | tf_op jit(solution)/shard_map/ppermute | solution.py:20
  138.1 3.4 %copy.67 = f32[4,32,36,2]{3,1,2,0:T(8,128)} copy(f32[4,32,36,2]{2,1,3,0:T(8,128)S(1)} %collective-permute-done.13) | data formatting | bytes 73728 | tf_op jit(solution)/shard_map/ppermute | solution.py:23
  141.4 4.1 %maximum_maximum_fusion.1 = (f32[4,32,36,130]{3,1,2,0:T(8,128)S(1)}, f32[4,32,36,130]{3,1,2,0:T(8,128)S(1)}) fusion(f32[4,32,2,128]{3,1,2,0:T(8,128)S(1)} %broadcast_select_fusion, f32[4,32,32,128]{3,1,2,0:T(8,128)S(1)} %fusion.7, f32[4,32,2,128]{3,1,2,0:T(8,128)S(1)} %collective-permute-done.7, f32[4,32,36,2]{3,1,2,0:T(8,128)} %copy.65, ...), kind=kLoop, calls=%fused_computation.5 | loop fusion | flops 3594240 | bytes 7225344 | tf_op jit(solution)/shard_map/concatenate | solution.py:24
  145.5 2.5 %multiply_subtract_fusion = f32[4,32,32,129]{3,1,2,0:T(8,128)S(1)} fusion(f32[4,32,36,130]{3,1,2,0:T(8,128)S(1)} %get-tuple-element.28, f32[4,32,36,130]{3,1,2,0:T(8,128)S(1)} %get-tuple-element.27, f32[32,32,129]{2,0,1:T(8,128)S(1)} %copy-done.7, f32[32,32,129]{2,0,1:T(8,128)S(1)} %copy-done.8), kind=kLoop, calls=%fused_computation.7 | loop fusion | flops 6868992 | bytes 11624448 | tf_op jit(solution)/shard_map/sub | solution.py:30
  148.1 0.9 fusion.4
  149.0 1.2 copy.71
  150.3 3.0 %copy.80 = f32[16,8,32,128]{3,1,2,0:T(8,128)} copy(f32[16,8,32,128]{3,2,1,0:T(8,128)S(1)} %bitcast.29) | data formatting | bytes 4194304
  153.3 2.9 %copy.69 = f32[128,4096]{0,1:T(8,128)} copy(f32[128,4096]{1,0:T(8,128)} %bitcast.30) | data formatting | bytes 4194304 | tf_op jit(solution)/shard_map/reshape | solution.py:108
  156.2 2.4 %scatter_custom_fusion = f32[128,128]{1,0:T(8,128)} fusion(s32[64]{0:T(128)} %fusion.14, f32[]{:T(128)} %constant.18.clone.1, f32[]{:T(128)} %constant.49.clone.1, pred[64]{0:T(512)(128)(4,1)S(1)} %copy-done.18, f32[128,4096]{0,1:T(8,128)} %copy.69, s32[1024]{0:T(1024)S(1)} %copy-done.17), kind=kCustom, calls=%fused_computation.53 | custom fusion | flops 8192 | bytes 2167872 | tf_op jit(solution)/shard_map/scatter | solution.py:118
  158.6 2.6 %all-to-all-start = ((f32[32,4,128]{2,1,0:T(4,128)}), f32[32,4,128]{2,1,0:T(4,128)S(1)}, u32[]{:S(2)}, u32[]{:S(2)}) async-start(f32[32,4,128]{2,1,0:T(4,128)} %bitcast.10), calls=%async_computation | async-start | bytes 131072 | tf_op jit(solution)/shard_map/all_to_all | solution.py:125
  161.2 1.2 convert_reduce_fusion.1
  162.4 6.1 %all-to-all-done = f32[32,4,128]{2,1,0:T(4,128)S(1)} async-done(((f32[32,4,128]{2,1,0:T(4,128)}), f32[32,4,128]{2,1,0:T(4,128)S(1)}, u32[]{:S(2)}, u32[]{:S(2)}) %all-to-all-start) | async-done | bytes 65568 | tf_op jit(solution)/shard_map/all_to_all | solution.py:125
  168.5 0.6 copy.82
  (69 shorter events, 0.6 us)
Async XLA Ops:
  0.6 2.9 %copy-start.15 = (s32[32,32,128]{2,1,0:T(8,128)S(1)}, s32[32,32,128]{2,1,0:T(8,128)}, u32[]{:S(2)}) copy-start(s32[32,32,128]{2,1,0:T(8,128)} %param.10) | copy-start | bytes 1572868
  3.8 20.2 %copy-start.19 = (s32[64,1]{0,1:T(1,128)S(1)}, s32[64,1]{0,1:T(1,128)}, u32[]{:S(2)}) copy-start(s32[64,1]{0,1:T(1,128)} %param.13) | copy-start | bytes 772
  4.0 7.2 %collective-permute-start.1 = (f32[5,32,2,128]{3,1,2,0:T(8,128)S(1)}, f32[5,32,2,128]{3,1,2,0:T(8,128)S(1)}, u32[]{:S(2)}, u32[]{:S(2)}) collective-permute-start(f32[5,32,2,128]{3,1,2,0:T(8,128)S(1)} %rev.8), channel_id=1, source_target_pairs={{0,1},{1,0},{2,3},{3,2},{4,5},{5,4},{6,7},{7,6},{8,9},{9,8},{10,11... | collective-permute-start | bytes 491528 | tf_op jit(solution)/shard_map/ppermute | solution.py:10
  11.2 10.2 %collective-permute-start.2 = (f32[5,32,2,128]{3,1,2,0:T(8,128)S(1)}, f32[5,32,2,128]{3,1,2,0:T(8,128)}, u32[]{:S(2)}, u32[]{:S(2)}) collective-permute-start(f32[5,32,2,128]{3,1,2,0:T(8,128)S(1)} %collective-permute-done.1), channel_id=1, source_target_pairs={{0,2},{1,3},{2,0},{3,1},{4,6},{5,7},{6,4},{7,5},{8,10},{9,11},{10,... | collective-permute-start | bytes 491528 | tf_op jit(solution)/shard_map/ppermute | solution.py:10
  14.8 0.8 copy-start.2
  16.4 16.3 %collective-permute-start.4 = (f32[7,32,2,128]{3,1,2,0:T(8,128)S(1)}, f32[7,32,2,128]{3,1,2,0:T(8,128)}, u32[]{:S(2)}, u32[]{:S(2)}) collective-permute-start(f32[7,32,2,128]{3,1,2,0:T(8,128)S(1)} %get-tuple-element.26), channel_id=1, source_target_pairs={{8,0},{16,8},{24,16},{9,1},{17,9},{25,17},{10,2},{18,10},{26,18},{... | collective-permute-start | bytes 688136 | tf_op jit(solution)/shard_map/ppermute | solution.py:23
  17.7 16.1 %collective-permute-start = (f32[7,32,2,128]{3,1,2,0:T(8,128)}, f32[7,32,2,128]{3,1,2,0:T(8,128)}, u32[]{:S(2)}, u32[]{:S(2)}) collective-permute-start(f32[7,32,2,128]{3,1,2,0:T(8,128)} %get-tuple-element.25), channel_id=1, source_target_pairs={{0,8},{8,16},{16,24},{1,9},{9,17},{17,25},{2,10},{10,18},{18,26},{... | collective-permute-start | bytes 688136 | tf_op jit(solution)/shard_map/ppermute | solution.py:20
  21.4 11.3 %collective-permute-start.3 = (f32[5,32,2,128]{3,1,2,0:T(8,128)}, f32[5,32,2,128]{3,1,2,0:T(8,128)S(1)}, u32[]{:S(2)}, u32[]{:S(2)}) collective-permute-start(f32[5,32,2,128]{3,1,2,0:T(8,128)} %collective-permute-done.2), channel_id=1, source_target_pairs={{0,4},{1,5},{2,6},{3,7},{4,0},{5,1},{6,2},{7,3},{8,12},{9,13},{10,... | collective-permute-start | bytes 491528 | tf_op jit(solution)/shard_map/ppermute | solution.py:10
  24.8 133.8 %all-to-all-start.1 = ((f32[32,1,1]{2,1,0:T(1,128)}), f32[32,1,1]{2,1,0:T(1,128)S(1)}, u32[]{:S(2)}, u32[]{:S(2)}) async-start(f32[32,1,1]{2,1,0:T(1,128)} %copy.70), calls=%async_computation.1 | async-start | bytes 32768 | tf_op jit(solution)/shard_map/all_to_all | solution.py:126
  44.2 13.6 %collective-permute-start.5 = (f32[7,32,36,2]{2,1,3,0:T(8,128)}, f32[7,32,36,2]{2,1,3,0:T(8,128)}, u32[]{:S(2)}, u32[]{:S(2)}) collective-permute-start(f32[7,32,36,2]{2,1,3,0:T(8,128)} %copy.57), channel_id=1, source_target_pairs={{0,1},{1,2},{2,3},{3,4},{4,5},{5,6},{6,7},{7,0},{8,9},{9,10},{10,1... | collective-permute-start | bytes 193544 | tf_op jit(solution)/shard_map/ppermute | solution.py:20
  49.9 12.1 %collective-permute-start.6 = (f32[7,32,36,2]{2,1,3,0:T(8,128)}, f32[7,32,36,2]{2,1,3,0:T(8,128)}, u32[]{:S(2)}, u32[]{:S(2)}) collective-permute-start(f32[7,32,36,2]{2,1,3,0:T(8,128)} %copy.58), channel_id=1, source_target_pairs={{1,0},{2,1},{3,2},{4,3},{5,4},{6,5},{7,6},{0,7},{9,8},{10,9},{11,1... | collective-permute-start | bytes 193544 | tf_op jit(solution)/shard_map/ppermute | solution.py:23
  77.9 4.0 %copy-start.16 = (f32[32,128]{1,0:T(8,128)S(1)}, f32[32,128]{1,0:T(8,128)}, u32[]{:S(2)}) copy-start(f32[32,128]{1,0:T(8,128)} %param.11) | copy-start | bytes 49156
  78.2 4.8 %copy-start = (f32[7,32,36,2]{3,1,2,0:T(8,128)S(1)}, f32[7,32,36,2]{3,1,2,0:T(8,128)}, u32[]{:S(2)}) copy-start(f32[7,32,36,2]{3,1,2,0:T(8,128)} %copy.59) | copy-start | bytes 193540
  78.2 4.8 %copy-start.1 = (f32[7,32,36,2]{3,1,2,0:T(8,128)S(1)}, f32[7,32,36,2]{3,1,2,0:T(8,128)}, u32[]{:S(2)}) copy-start(f32[7,32,36,2]{3,1,2,0:T(8,128)} %copy.60) | copy-start | bytes 193540
  78.2 4.8 %copy-start.3 = (f32[1,32,32,128]{3,1,2,0:T(8,128)S(1)}, f32[1,32,32,128]{3,1,2,0:T(8,128)}, u32[]{:S(2)}) copy-start(f32[1,32,32,128]{3,1,2,0:T(8,128)} %copy-done.2) | copy-start | bytes 1572868
  92.6 4.1 %copy-start.5 = (f32[7,32,34,128]{3,1,2,0:T(8,128)S(1)}, f32[7,32,34,128]{3,1,2,0:T(8,128)}, u32[]{:S(2)}) copy-start(f32[7,32,34,128]{3,1,2,0:T(8,128)} %get-tuple-element.23) | copy-start | bytes 11698180
  92.6 4.1 %copy-start.6 = (f32[7,32,34,128]{3,1,2,0:T(8,128)S(1)}, f32[7,32,34,128]{3,1,2,0:T(8,128)}, u32[]{:S(2)}) copy-start(f32[7,32,34,128]{3,1,2,0:T(8,128)} %get-tuple-element.24) | copy-start | bytes 11698180
  92.7 4.1 %copy-start.11 = (f32[32,33,128]{2,0,1:T(8,128)S(1)}, f32[32,33,128]{2,0,1:T(8,128)}, u32[]{:S(2)}) copy-start(f32[32,33,128]{2,0,1:T(8,128)} %get-tuple-element.14) | copy-start | bytes 1622020
  92.7 4.1 %copy-start.12 = (f32[32,33,128]{2,0,1:T(8,128)S(1)}, f32[32,33,128]{2,0,1:T(8,128)}, u32[]{:S(2)}) copy-start(f32[32,33,128]{2,0,1:T(8,128)} %get-tuple-element.15) | copy-start | bytes 1622020
  96.8 1.6 copy-start.9
  96.8 1.7 copy-start.13
  98.5 2.2 %copy-start.20 = (s32[64,1]{0,1:T(1,128)S(1)}, s32[64,1]{0,1:T(1,128)}, u32[]{:S(2)}) copy-start(s32[64,1]{0,1:T(1,128)} %param.13) | copy-start | bytes 772
  98.5 2.2 %copy-start.22 = (s32[64]{0:T(128)S(1)}, s32[64]{0:T(128)}, u32[]{:S(2)}) copy-start(s32[64]{0:T(128)} %convert_reduce_fusion) | copy-start | bytes 772
  98.5 7.2 %copy-start.21 = (s32[64]{0:T(128)S(1)}, s32[64]{0:T(128)}, u32[]{:S(2)}) copy-start(s32[64]{0:T(128)} %param.12) | copy-start | bytes 772
  100.6 5.0 %collective-permute-start.8 = (f32[4,32,2,128]{3,1,2,0:T(8,128)S(1)}, f32[4,32,2,128]{3,1,2,0:T(8,128)S(1)}, u32[]{:S(2)}, u32[]{:S(2)}) collective-permute-start(f32[4,32,2,128]{3,1,2,0:T(8,128)S(1)} %rev.9), channel_id=1, source_target_pairs={{0,1},{1,0},{2,3},{3,2},{4,5},{5,4},{6,7},{7,6},{8,9},{9,8},{10,11... | collective-permute-start | bytes 393224 | tf_op jit(solution)/shard_map/ppermute | solution.py:10
  105.7 5.0 %collective-permute-start.9 = (f32[4,32,2,128]{3,1,2,0:T(8,128)S(1)}, f32[4,32,2,128]{3,1,2,0:T(8,128)S(1)}, u32[]{:S(2)}, u32[]{:S(2)}) collective-permute-start(f32[4,32,2,128]{3,1,2,0:T(8,128)S(1)} %collective-permute-done.8), channel_id=1, source_target_pairs={{0,2},{1,3},{2,0},{3,1},{4,6},{5,7},{6,4},{7,5},{8,10},{9,11},{10,... | collective-permute-start | bytes 393224 | tf_op jit(solution)/shard_map/ppermute | solution.py:10
  105.7 7.3 %collective-permute-start.11 = (f32[4,32,2,128]{3,1,2,0:T(8,128)S(1)}, f32[4,32,2,128]{3,1,2,0:T(8,128)S(1)}, u32[]{:S(2)}, u32[]{:S(2)}) collective-permute-start(f32[4,32,2,128]{3,1,2,0:T(8,128)S(1)} %get-tuple-element.31), channel_id=1, source_target_pairs={{8,0},{16,8},{24,16},{9,1},{17,9},{25,17},{10,2},{18,10},{26,18},{... | collective-permute-start | bytes 393224 | tf_op jit(solution)/shard_map/ppermute | solution.py:23
  110.6 6.7 %collective-permute-start.10 = (f32[4,32,2,128]{3,1,2,0:T(8,128)S(1)}, f32[4,32,2,128]{3,1,2,0:T(8,128)S(1)}, u32[]{:S(2)}, u32[]{:S(2)}) collective-permute-start(f32[4,32,2,128]{3,1,2,0:T(8,128)S(1)} %collective-permute-done.9), channel_id=1, source_target_pairs={{0,4},{1,5},{2,6},{3,7},{4,0},{5,1},{6,2},{7,3},{8,12},{9,13},{10,... | collective-permute-start | bytes 393224 | tf_op jit(solution)/shard_map/ppermute | solution.py:10
  111.7 5.6 %collective-permute-start.7 = (f32[4,32,2,128]{3,1,2,0:T(8,128)S(1)}, f32[4,32,2,128]{3,1,2,0:T(8,128)S(1)}, u32[]{:S(2)}, u32[]{:S(2)}) collective-permute-start(f32[4,32,2,128]{3,1,2,0:T(8,128)S(1)} %get-tuple-element.32), channel_id=1, source_target_pairs={{0,8},{8,16},{16,24},{1,9},{9,17},{17,25},{2,10},{10,18},{18,26},{... | collective-permute-start | bytes 393224 | tf_op jit(solution)/shard_map/ppermute | solution.py:20
  123.6 11.2 %collective-permute-start.12 = (f32[4,32,36,2]{2,1,3,0:T(8,128)S(1)}, f32[4,32,36,2]{2,1,3,0:T(8,128)S(1)}, u32[]{:S(2)}, u32[]{:S(2)}) collective-permute-start(f32[4,32,36,2]{2,1,3,0:T(8,128)S(1)} %copy.64), channel_id=1, source_target_pairs={{0,1},{1,2},{2,3},{3,4},{4,5},{5,6},{6,7},{7,0},{8,9},{9,10},{10,1... | collective-permute-start | bytes 110600 | tf_op jit(solution)/shard_map/ppermute | solution.py:20
  126.7 11.3 %collective-permute-start.13 = (f32[4,32,36,2]{2,1,3,0:T(8,128)S(1)}, f32[4,32,36,2]{2,1,3,0:T(8,128)S(1)}, u32[]{:S(2)}, u32[]{:S(2)}) collective-permute-start(f32[4,32,36,2]{2,1,3,0:T(8,128)S(1)} %copy.66), channel_id=1, source_target_pairs={{1,0},{2,1},{3,2},{4,3},{5,4},{6,5},{7,6},{0,7},{9,8},{10,9},{11,1... | collective-permute-start | bytes 110600 | tf_op jit(solution)/shard_map/ppermute | solution.py:23
  141.4 4.1 %copy-start.7 = (f32[32,32,129]{2,0,1:T(8,128)S(1)}, f32[32,32,129]{2,0,1:T(8,128)}, u32[]{:S(2)}) copy-start(f32[32,32,129]{2,0,1:T(8,128)} %get-tuple-element.12) | copy-start | bytes 1585156
  141.4 4.1 %copy-start.8 = (f32[32,32,129]{2,0,1:T(8,128)S(1)}, f32[32,32,129]{2,0,1:T(8,128)}, u32[]{:S(2)}) copy-start(f32[32,32,129]{2,0,1:T(8,128)} %get-tuple-element.13) | copy-start | bytes 1585156
  145.5 2.6 %copy-start.4 = (f32[4,32,33,128]{3,1,2,0:T(8,128)S(1)}, f32[4,32,33,128]{3,1,2,0:T(8,128)}, u32[]{:S(2)}) copy-start(f32[4,32,33,128]{3,1,2,0:T(8,128)} %multiply_subtract_fusion.2) | copy-start | bytes 6488068
  145.5 2.6 %copy-start.14 = (f32[32,32,128]{2,0,1:T(8,128)S(1)}, f32[32,32,128]{2,0,1:T(8,128)}, u32[]{:S(2)}) copy-start(f32[32,32,128]{2,0,1:T(8,128)} %slice_multiply_fusion.4) | copy-start | bytes 1572868
  150.2 6.0 %copy-start.10 = (f32[4,32,32,128]{3,2,1,0:T(8,128)}, f32[4,32,32,128]{3,2,1,0:T(8,128)S(1)}, u32[]{:S(2)}) copy-start(f32[4,32,32,128]{3,2,1,0:T(8,128)S(1)} %copy.71) | copy-start | bytes 6291460
  150.2 5.9 %copy-start.17 = (s32[1024]{0:T(1024)S(1)}, s32[1024]{0:T(1024)}, u32[]{:S(2)}) copy-start(s32[1024]{0:T(1024)} %pad_clamp_fusion) | copy-start | bytes 12292
  150.3 5.9 %copy-start.18 = (pred[64]{0:T(512)(128)(4,1)S(1)}, pred[64]{0:T(512)(128)(4,1)}, u32[]{:S(2)}) copy-start(pred[64]{0:T(512)(128)(4,1)} %compare_and_fusion) | copy-start | bytes 196
  158.6 9.9 %all-to-all-start = ((f32[32,4,128]{2,1,0:T(4,128)}), f32[32,4,128]{2,1,0:T(4,128)S(1)}, u32[]{:S(2)}, u32[]{:S(2)}) async-start(f32[32,4,128]{2,1,0:T(4,128)} %bitcast.10), calls=%async_computation | async-start | bytes 131072 | tf_op jit(solution)/shard_map/all_to_all | solution.py:125
where the time goes:
time: 170 us; the launch traced here: 169 us
  other arithmetic  59.2 us (35%)
  local copies, waits for them, and re-layouts  52.5 us (31%)
  starting transfers between devices  30.1 us (18%)
  waiting for transfers between devices  26.2 us (15%)
    concatenate x3, other arithmetic, padded(): block = jnp.concatenate([low, block, high], axis=dim)  25.3 us
    ppermute x6, waiting for transfers between devices, partner(): lax.ppermute(shard, axis, [(i, i ^ 1 << stride) for i in range(lax.axis_s...  20 us
    slice x4, local copies, waits for them, and re-layouts, padded(): lax.slice_in_dim(block, block.shape[dim] - width, None, axis=dim)  14.9 us
    sub x4, other arithmetic, face_flux(): velocity * (7.0 * (current + forward) - (behind + farther)) / 12.0  10.9 us
    ppermute x4, starting transfers between devices, padded(): lax.ppermute(lax.slice_in_dim(block, 0, width, axis=dim), axis, backward)  10.4 us
    unnamed x50, local copies, waits for them, and re-layouts  9.32 us
    ppermute x2, local copies, waits for them, and re-layouts, padded(): lax.ppermute(lax.slice_in_dim(block, 0, width, axis=dim), axis, backward)  7.61 us
    ppermute x2, local copies, waits for them, and re-layouts, padded(): lax.ppermute(lax.slice_in_dim(block, block.shape[dim] - width, None, axis...  7.52 us
  transfers between devices with their start and end apart: 16, of which 6 were waited for; matrix products, arithmetic and copies ran while one was open for 63% of the time, Pallas kernels for 0%

commit v1 on v0

v1 whole, which is shorter than its diff:
```python
import functools

import jax
import jax.numpy as jnp
from jax import lax
from jax.experimental import pallas as pl
from jax.experimental.pallas import tpu as pltpu
from jax.sharding import PartitionSpec as P

CAP = 4
BOX = 8
PADR = 8
MESH = pl.DeviceIdType.MESH


def kernel(
    dims, area_h, cell_h, owner_h, mask_h, east_h, north_h, tracers_h, out_h, arrivals, counts,
    area, cell, owner, mask, east, north, first, second, final, wet, flow, coef,
    cols, send_l, send_r, get_l, get_r, send_n, send_s, get_n, get_s,
    pick, halves, outbox, inbox,
    in_sem, out_sem, halo_send, halo_recv, box_send, box_recv,
):
    tracer_count, levels, rows, n_lat, n_lon = dims
    planes = tracer_count * levels
    tall = rows + 2 * PADR
    n_dev = n_lat * n_lon
    slots = n_dev * BOX
    floats = cell.shape[1]
    lat, lon = lax.axis_index("lat"), lax.axis_index("lon")
    me = lat * n_lon + lon
    top = lat == n_lat - 1
    bottom = lat == 0

    loads = [
        pltpu.make_async_copy(mask_h, mask, in_sem.at[0]),
        pltpu.make_async_copy(east_h, east, in_sem.at[1]),
        pltpu.make_async_copy(north_h, north, in_sem.at[2]),
        pltpu.make_async_copy(tracers_h, first.at[:, pl.ds(PADR, rows), :], in_sem.at[3]),
        pltpu.make_async_copy(area_h, area, in_sem.at[4]),
        pltpu.make_async_copy(cell_h, cell, in_sem.at[5]),
        pltpu.make_async_copy(owner_h, owner, in_sem.at[6]),
    ]
    for load in loads:
        load.start()

    barrier = pltpu.get_barrier_semaphore()

    def greet(j, carry):
        other = lax.rem(me + j, n_dev)
        pl.semaphore_signal(
            barrier, inc=1, device_id=(other // n_lon, lax.rem(other, n_lon)), device_id_type=MESH
        )
        return carry

    lax.fori_loop(1, n_dev, greet, 0)

    lane = lax.broadcasted_iota(jnp.int32, (8, 128), 1)
    group = lane // 4
    low_pair = lax.rem(lane, 4) < 2
    lane_all = lax.broadcasted_iota(jnp.int32, (rows, 128), 1)
    low_all = lax.rem(lane_all, 4) < 2
    groups = rows // 8

    for load in loads[:4]:
        load.wait()

    def gather_columns(k, acc):
        acc = list(acc)
        here = group == k
        for g in range(groups):
            at = pl.ds(PADR + 8 * g, 8)
            sub = pl.ds(8 * g, 8)
            water = mask[k, sub, :].astype(jnp.float32)
            wet[k, at, :] = water
            flow[k, at, :] = north[k, sub, :] * water
            edge = jnp.where(lane == 0, water, east[k, sub, :] * water)
            values = [first[c * levels + k, at, :] for c in range(tracer_count)] + [edge]
            for c, value in enumerate(values):
                i = c * groups + g
                acc[i] = jnp.where(here, pltpu.roll(value, 4 * k + 2, 1), acc[i])
        return tuple(acc)

    blank = jnp.zeros((8, 128), jnp.float32)
    packed = lax.fori_loop(0, levels, gather_columns, (blank,) * ((tracer_count + 1) * groups))

    def fill_columns(packed, step):
        for pair in range(tracer_count // 2):
            for g in range(groups):
                a, b = packed[2 * pair * groups + g], packed[(2 * pair + 1) * groups + g]
                sub = pl.ds(pair * rows + 8 * g, 8)
                send_r[step, sub, :] = jnp.where(low_pair, a, pltpu.roll(b, 2, 1))
                send_l[step, sub, :] = jnp.where(low_pair, pltpu.roll(b, 126, 1), a)
        if step == 0:
            for g in range(groups):
                value = packed[tracer_count * groups + g]
                sub = pl.ds(tracer_count // 2 * rows + 8 * g, 8)
                send_r[step, sub, :] = value
                send_l[step, sub, :] = value

    def fill_rows(field, step):
        flat = field.reshape(planes * tall, 128)
        wet_flat = wet.reshape(levels * tall, 128)
        flow_flat = flow.reshape(levels * tall, 128)

        def row(r):
            return flat[pl.ds(PADR + r, planes, stride=tall), :]

        @pl.when(jnp.logical_not(top))
        def _():
            send_n[step, pl.ds(0, planes), :] = row(rows - 2)
            send_n[step, pl.ds(planes, planes), :] = row(rows - 1)
            if step == 0:
                send_n[step, pl.ds(2 * planes, levels), :] = flow_flat[
                    pl.ds(PADR + rows - 1, levels, stride=tall), :
                ]

        @pl.when(top)
        def _():
            ahead = lax.broadcasted_iota(jnp.int32, (128, 128), 0)
            across = lax.broadcasted_iota(jnp.int32, (128, 128), 1)
            turn = (ahead + across == 127).astype(jnp.float32)

            def turned(value):
                return jnp.dot(
                    value, turn, precision=lax.Precision.HIGHEST, preferred_element_type=jnp.float32
                )

            send_n[step, pl.ds(0, planes), :] = turned(row(rows - 1))
            send_n[step, pl.ds(planes, planes), :] = turned(row(rows - 2))
            if step == 0:
                send_n[step, pl.ds(2 * planes, levels), :] = turned(
                    wet_flat[pl.ds(PADR + rows - 1, levels, stride=tall), :]
                )

        send_s[step, pl.ds(0, planes), :] = row(0)
        send_s[step, pl.ds(planes, planes), :] = row(1)
        if step == 0:
            send_s[step, pl.ds(2 * planes, levels), :] = wet_flat[
                pl.ds(PADR, levels, stride=tall), :
            ]

    right, left = lax.rem(lon + 1, n_lon), lax.rem(lon + n_lon - 1, n_lon)
    upper = (jnp.where(top, lat, lat + 1), jnp.where(top, n_lon - 1 - lon, lon))
    lower = (jnp.where(bottom, 0, lat - 1), lon)

    def halo_copies(step):
        row_size = 2 * planes + (levels if step == 0 else 0)
        col_size = tracer_count // 2 * rows + (rows if step == 0 else 0)
        plan = (
            (send_r, get_l, col_size, (lat, right)),
            (send_l, get_r, col_size, (lat, left)),
            (send_n, get_s, row_size, upper),
            (send_s, get_n, row_size, lower),
        )
        return [
            pltpu.make_async_remote_copy(
                src_ref=source.at[step, pl.ds(0, size)],
                dst_ref=target.at[step, pl.ds(0, size)],
                send_sem=halo_send.at[step, i],
                recv_sem=halo_recv.at[step, i],
                device_id=device,
                device_id_type=MESH,
            )
            for i, (source, target, size, device) in enumerate(plan)
        ]

    def start_halos(step):
        east_copy, west_copy, up_copy, down_copy = halo_copies(step)
        row_size = 2 * planes + (levels if step == 0 else 0)
        fold_copy = pltpu.make_async_remote_copy(
            src_ref=send_n.at[step, pl.ds(0, row_size)],
            dst_ref=get_n.at[step, pl.ds(0, row_size)],
            send_sem=halo_send.at[step, 2],
            recv_sem=halo_recv.at[step, 3],
            device_id=upper,
            device_id_type=MESH,
        )

        @pl.when(jnp.logical_not(top))
        def _():
            up_copy.start()

        @pl.when(top)
        def _():
            fold_copy.start()

        @pl.when(jnp.logical_not(bottom))
        def _():
            down_copy.start()

        east_copy.start()
        west_copy.start()

    def wait_halos(step):
        east_copy, west_copy, up_copy, down_copy = halo_copies(step)
        east_copy.wait()
        west_copy.wait()
        up_copy.wait_send()
        down_copy.wait_recv()

        @pl.when(jnp.logical_not(bottom))
        def _():
            down_copy.wait_send()
            up_copy.wait_recv()

    def place_halos(field, step):
        flat = field.reshape(planes * tall, 128)
        wet_flat = wet.reshape(levels * tall, 128)
        flow_flat = flow.reshape(levels * tall, 128)
        for i in range(2):
            flat[pl.ds(PADR + rows + i, planes, stride=tall), :] = get_n[
                step, pl.ds(i * planes, planes), :
            ]
        if step == 0:
            wet_flat[pl.ds(PADR + rows, levels, stride=tall), :] = get_n[
                step, pl.ds(2 * planes, levels), :
            ]

        @pl.when(bottom)
        def _():
            for i in range(2):
                flat[pl.ds(PADR - 2 + i, planes, stride=tall), :] = jnp.zeros((planes, 128), jnp.float32)
            if step == 0:
                flow_flat[pl.ds(PADR - 1, levels, stride=tall), :] = jnp.zeros((levels, 128), jnp.float32)

        @pl.when(jnp.logical_not(bottom))
        def _():
            for i in range(2):
                flat[pl.ds(PADR - 2 + i, planes, stride=tall), :] = get_s[
                    step, pl.ds(i * planes, planes), :
                ]
            if step == 0:
                flow_flat[pl.ds(PADR - 1, levels, stride=tall), :] = get_s[
                    step, pl.ds(2 * planes, levels), :
                ]

        for pair in range(tracer_count // 2):
            from_l = get_l[step, pl.ds(pair * rows, rows), :]
            from_r = get_r[step, pl.ds(pair * rows, rows), :]
            cols[2 * pair] = jnp.where(low_all, from_l, from_r)
            cols[2 * pair + 1] = jnp.where(
                low_all, pltpu.roll(from_l, 126, 1), pltpu.roll(from_r, 2, 1)
            )
        if step == 0:
            sub = pl.ds(tracer_count // 2 * rows, rows)
            cols[tracer_count] = jnp.where(low_all, get_l[step, sub, :], get_r[step, sub, :])

    def make_coefficients(k, g):
        at = pl.ds(PADR + 8 * g, 8)
        sub = pl.ds(8 * g, 8)
        beside = pltpu.roll(cols[tracer_count, sub, :], 126 - 4 * k, 1)
        water = wet[k, at, :]
        scale = area[sub, :] * water * (1.0 / 6.0)
        stream = east[k, sub, :] * water
        face_e = stream * pltpu.roll(jnp.where(lane == 0, beside, water), 127, 1)
        face_w = pltpu.roll(jnp.where(lane == 127, beside, stream), 1, 1) * water
        face_n = flow[k, at, :] * wet[k, pl.ds(PADR + 8 * g + 1, 8), :]
        face_s = flow[k, pl.ds(PADR + 8 * g - 1, 8), :] * water
        made = []
        centre = 1.0
        for ahead, behind in ((face_e, face_w), (face_n, face_s)):
            pos, neg = jnp.maximum(ahead, 0.0) * scale, jnp.minimum(ahead, 0.0) * scale
            pos_b, neg_b = jnp.maximum(behind, 0.0) * scale, jnp.minimum(behind, 0.0) * scale
            centre = centre - (5.0 * (pos - neg_b) + 2.0 * (neg - pos_b))
            made += [
                -pos_b,
                pos + 5.0 * pos_b + 2.0 * neg_b,
                -(2.0 * pos + 5.0 * neg + neg_b),
                neg,
            ]
        return [centre] + made

    def apply(field, k, g, c, weights):
        centre, xm2, xm1, xp1, xp2, ym2, ym1, yp1, yp2 = weights
        plane = c * levels + k
        base = PADR + 8 * g
        value = field[plane, pl.ds(base, 8), :]
        beside = pltpu.roll(cols[c, pl.ds(8 * g, 8), :], 126 - 4 * k, 1)
        total = centre * value
        total += xm2 * pltpu.roll(jnp.where(lane >= 126, beside, value), 2, 1)
        total += xm1 * pltpu.roll(jnp.where(lane == 127, beside, value), 1, 1)
        total += xp1 * pltpu.roll(jnp.where(lane == 0, beside, value), 127, 1)
        total += xp2 * pltpu.roll(jnp.where(lane <= 1, beside, value), 126, 1)
        total += ym2 * field[plane, pl.ds(base - 2, 8), :]
        total += ym1 * field[plane, pl.ds(base - 1, 8), :]
        total += yp1 * field[plane, pl.ds(base + 1, 8), :]
        total += yp2 * field[plane, pl.ds(base + 2, 8), :]
        return total

    def first_step(k, acc):
        acc = list(acc)
        here = group == k
        for g in range(groups):
            weights = make_coefficients(k, g)
            for n, weight in enumerate(weights):
                coef[k, n, pl.ds(8 * g, 8), :] = weight
            for c in range(tracer_count):
                value = apply(first, k, g, c, weights)
                second[c * levels + k, pl.ds(PADR + 8 * g, 8), :] = value
                i = c * groups + g
                acc[i] = jnp.where(here, pltpu.roll(value, 4 * k + 2, 1), acc[i])
        return tuple(acc)

    def second_step(k, carry):
        for g in range(groups):
            weights = [coef[k, n, pl.ds(8 * g, 8), :] for n in range(9)]
            for c in range(tracer_count):
                final[c * levels + k, pl.ds(8 * g, 8), :] = apply(second, k, g, c, weights)
        return carry

    fill_columns(packed, 0)
    fill_rows(first, 0)
    pl.semaphore_wait(barrier, n_dev - 1)
    start_halos(0)

    for load in loads[4:]:
        load.wait()
    cell_row, owner_row = cell[...], owner[...]
    f_row = lax.broadcasted_iota(jnp.int32, (floats, floats), 0)
    f_col = lax.broadcasted_iota(jnp.int32, (floats, floats), 1)
    diagonal = f_row == f_col
    owner_f = owner_row.astype(jnp.float32)
    owner_col = jnp.sum(jnp.where(diagonal, owner_f, 0.0), axis=1, keepdims=True)
    cell_col = jnp.sum(jnp.where(diagonal, cell_row.astype(jnp.float32), 0.0), axis=1, keepdims=True)
    rank = jnp.sum(
        jnp.where((owner_col == owner_f) & (f_col < f_row), 1.0, 0.0), axis=1, keepdims=True
    )
    slot_col = owner_col * float(BOX) + rank
    slot_lane = lax.broadcasted_iota(jnp.int32, (floats, slots), 1).astype(jnp.float32)
    wanted = jnp.sum(jnp.where(slot_col == slot_lane, cell_col + 1.0, 0.0), axis=0, keepdims=True) - 1.0
    wanted = wanted.astype(jnp.int32)
    slot_row = lax.broadcasted_iota(jnp.int32, (slots, floats), 0)
    tally = jnp.sum(
        jnp.where(owner_row * BOX + CAP == slot_row, 1.0, 0.0), axis=1, keepdims=True
    )

    def mark(r, carry):
        start = pl.multiple_of(r * 128, 128)
        place = lax.broadcasted_iota(jnp.int32, (128, slots), 0) + start
        pick[pl.ds(start, 128), :] = jnp.where(place == wanted, 1.0, 0.0).astype(jnp.bfloat16)
        return carry

    lax.fori_loop(0, rows, mark, 0)

    wait_halos(0)
    place_halos(first, 0)
    packed = lax.fori_loop(0, levels, first_step, (blank,) * (tracer_count * groups))
    fill_columns(packed, 1)
    fill_rows(second, 1)
    start_halos(1)
    wait_halos(1)
    place_halos(second, 1)
    lax.fori_loop(0, levels, second_step, 0)
    store = pltpu.make_async_copy(final, out_h, out_sem.at[0])
    store.start()

    flat = final.reshape(planes * rows, 128)
    for r in range(rows):
        value = flat[pl.ds(r, planes, stride=rows), :]
        high = value.astype(jnp.bfloat16)
        rest = (value - high.astype(jnp.float32)).astype(jnp.bfloat16)
        halves[pl.ds(0, planes), pl.ds(r * 128, 128)] = high
        halves[pl.ds(planes, planes), pl.ds(r * 128, 128)] = rest
    taken = jnp.dot(halves[...], pick[...], preferred_element_type=jnp.float32)
    outbox[...] = jnp.transpose(taken[:planes] + taken[planes:]) + tally

    def box_copy(j):
        other = lax.rem(me + j, n_dev)
        return pltpu.make_async_remote_copy(
            src_ref=outbox.at[pl.ds(pl.multiple_of(other * BOX, BOX), BOX)],
            dst_ref=inbox.at[pl.ds(pl.multiple_of(me * BOX, BOX), BOX)],
            send_sem=box_send.at[other],
            recv_sem=box_recv.at[me],
            device_id=(other // n_lon, lax.rem(other, n_lon)),
            device_id_type=MESH,
        )

    def box_start(j, carry):
        box_copy(j).start()
        return carry

    def box_wait(j, carry):
        other = lax.rem(me + j, n_dev)
        at = pl.ds(pl.multiple_of(other * BOX, BOX), BOX)
        copy = pltpu.make_async_remote_copy(
            src_ref=outbox.at[at],
            dst_ref=inbox.at[at],
            send_sem=box_send.at[other],
            recv_sem=box_recv.at[other],
            device_id=(other // n_lon, lax.rem(other, n_lon)),
            device_id_type=MESH,
        )
        copy.wait()
        return carry

    lax.fori_loop(1, n_dev, box_start, 0)
    own = pl.ds(pl.multiple_of(me * BOX, BOX), BOX)
    inbox[own, :] = outbox[own, :]
    lax.fori_loop(1, n_dev, box_wait, 0)
    for i in range(CAP):
        arrivals[pl.ds(i, n_dev, stride=CAP), :] = inbox[pl.ds(i, n_dev, stride=BOX), :]
    told = inbox[pl.ds(CAP, n_dev, stride=BOX), :][:, :n_dev]
    straight = lax.broadcasted_iota(jnp.int32, (n_dev, n_dev), 0) == lax.broadcasted_iota(
        jnp.int32, (n_dev, n_dev), 1
    )
    counts[...] = jnp.sum(jnp.where(straight, told, 0.0), axis=0, keepdims=True).astype(jnp.int32)
    store.wait()


def local(tracers, vel_east, vel_north, land_mask, step_area, float_cell, float_owner):
    tracer_count, levels, rows, columns = tracers.shape
    n_lat, n_lon = lax.axis_size("lat"), lax.axis_size("lon")
    n_dev = n_lat * n_lon
    planes = tracer_count * levels
    tall = rows + 2 * PADR
    floats = float_cell.shape[0]
    row_size = 2 * planes + levels
    col_size = (tracer_count // 2 + 1) * rows
    f32 = jnp.float32
    whole = pl.BlockSpec(memory_space=pl.ANY)
    vmem = pl.BlockSpec(memory_space=pltpu.VMEM)
    out, arrivals, counts = pl.pallas_call(
        functools.partial(kernel, (tracer_count, levels, rows, n_lat, n_lon)),
        out_shape=(
            jax.ShapeDtypeStruct((planes, rows, columns), f32),
            jax.ShapeDtypeStruct((n_dev * CAP, planes), f32),
            jax.ShapeDtypeStruct((1, n_dev), jnp.int32),
        ),
        in_specs=[whole] * 7,
        out_specs=(whole, vmem, vmem),
        scratch_shapes=[
            pltpu.VMEM((rows, columns), f32),
            pltpu.VMEM((1, floats), jnp.int32),
            pltpu.VMEM((1, floats), jnp.int32),
            pltpu.VMEM((levels, rows, columns), jnp.int32),
            pltpu.VMEM((levels, rows, columns), f32),
            pltpu.VMEM((levels, rows, columns), f32),
            pltpu.VMEM((planes, tall, columns), f32),
            pltpu.VMEM((planes, tall, columns), f32),
            pltpu.VMEM((planes, rows, columns), f32),
            pltpu.VMEM((levels, tall, columns), f32),
            pltpu.VMEM((levels, tall, columns), f32),
            pltpu.VMEM((levels, 9, rows, columns), f32),
            pltpu.VMEM((tracer_count + 1, rows, columns), f32),
            *[pltpu.VMEM((2, col_size, columns), f32)] * 4,
            *[pltpu.VMEM((2, row_size, columns), f32)] * 4,
            pltpu.VMEM((rows * columns, n_dev * BOX), jnp.bfloat16),
            pltpu.VMEM((2 * planes, rows * columns), jnp.bfloat16),
            pltpu.VMEM((n_dev * BOX, planes), f32),
            pltpu.VMEM((n_dev * BOX, planes), f32),
            pltpu.SemaphoreType.DMA((7,)),
            pltpu.SemaphoreType.DMA((1,)),
            pltpu.SemaphoreType.DMA((2, 4)),
            pltpu.SemaphoreType.DMA((2, 4)),
            pltpu.SemaphoreType.DMA((n_dev,)),
            pltpu.SemaphoreType.DMA((n_dev,)),
        ],
        compiler_params=pltpu.CompilerParams(
            collective_id=0, has_side_effects=True, vmem_limit_bytes=56 * 1024 * 1024
        ),
        cost_estimate=pl.CostEstimate(
            flops=2 * 17 * planes * rows * columns, bytes_accessed=8 * 1024 * 1024, transcendentals=0
        ),
    )(
        step_area,
        float_cell.reshape(1, floats),
        float_owner.reshape(1, floats),
        land_mask,
        vel_east,
        vel_north,
        tracers.reshape(planes, rows, columns),
    )
    return out.reshape(tracers.shape), arrivals, counts.reshape(n_dev)


def solution(mesh):
    placed = (
        P(None, None, "lat", "lon"),
        P(None, "lat", "lon"),
        P(None, "lat", "lon"),
        P(None, "lat", "lon"),
        P("lat", "lon"),
        P(("lat", "lon")),
        P(("lat", "lon"), None),
    )
    return jax.shard_map(
        local,
        mesh=mesh,
        in_specs=placed,
        out_specs=(P(None, None, "lat", "lon"), P(("lat", "lon"), None), P(("lat", "lon"))),
        check_vma=False,
    )
```

time: 170 us -> 49.7 us (0.29)
  other arithmetic: 59.2 us -> 0 us
  local copies, waits for them, and re-layouts: 52.5 us -> 4.26 us
  Pallas kernels: 0 us -> 44.7 us
  starting transfers between devices: 30.1 us -> 0 us
  waiting for transfers between devices: 26.2 us -> 0 us
    pallas_call x0 -> x1, Pallas kernels: none -> 44.7 us  [local(): pl.pallas_call(functools.partial(kernel, (tracer_count, levels, rows, n_l...]
    concatenate x7 -> x0, other arithmetic: 31.8 us -> none  [the longest x3 25.3 us: padded(): block = jnp.concatenate([low, block, high], axis=dim)]
    ppermute x14 -> x0, starting transfers between devices: 24.6 us -> none  [the longest x4 10.4 us: padded(): lax.ppermute(lax.slice_in_dim(block, 0, width, axis=dim), axis, backward)]
    slice x10 -> x0, local copies, waits for them, and re-layouts: 22.1 us -> none  [the longest x4 14.9 us: padded(): lax.slice_in_dim(block, block.shape[dim] - width, None, axis=dim)]
    ppermute x14 -> x0, waiting for transfers between devices: 20.1 us -> none  [the longest x6 20 us: partner(): lax.ppermute(shard, axis, [(i, i ^ 1 << stride) for i in range(lax.axis_s...]
    ppermute x4 -> x0, local copies, waits for them, and re-layouts: 15.1 us -> none  [the longest x2 7.61 us: padded(): lax.ppermute(lax.slice_in_dim(block, 0, width, axis=dim), axis, backward)]
    sub x6 -> x0, other arithmetic: 13.8 us -> none  [the longest x4 10.9 us: face_flux(): velocity * (7.0 * (current + forward) - (behind + farther)) / 12.0]
    all_to_all x2 -> x0, waiting for transfers between devices: 6.1 us -> none  [the longest x1 6.1 us: local(): lax.all_to_all(outbox, ('lat', 'lon'), split_axis=0, concat_axis=0, tiled...]
  transfers between devices with their start and end apart: 16 -> 0, of which waited for: 6 -> 0; matrix products, arithmetic and copies ran while one was open for 63% -> 0% of each run, Pallas kernels for 0% -> 0%
where the time goes in v1:
time: 49.7 us; the launch traced here: 49.6 us
  Pallas kernels  44.7 us (90%)
  local copies, waits for them, and re-layouts  4.26 us (9%)
  between operations  0.66 us (1%)
    pallas_call x1, Pallas kernels, local(): pl.pallas_call(functools.partial(kernel, (tracer_count, levels, rows, n_l...  44.7 us
    unnamed x7, local copies, waits for them, and re-layouts  4.26 us

profile of v1, /device:TPU:0, one launch (start us, length us, event | category | flops | bytes accessed | tf_op | source)
XLA Modules:
  0.0 49.6 jit_solution(12950743567482690742)
XLA Ops:
  0.6 44.7 %shard_map.94 = (f32[128,32,128]{2,1,0:T(8,128)}, f32[128,128]{1,0:T(8,128)}, s32[1,32]{1,0:T(1,128)}) custom-call(f32[32,128]{1,0:T(8,128)} %area_h.1, s32[1,64]{1,0:T(1,128)} %bitcast.7, s32[1,64]{1,0:T(1,128)} %bitcast.8, s32[32,32,128]{2,1,0:T(8,128)} %mask_h.1, f32[32,32,128]{2,1,0:T(8,128)} %east_h.1, f32[32,32,128]{2,1,0:T(8,128)} %north_h.1, ...), custom_call_target="tpu_custom_call" | custom-call | flops 17825792 | bytes 8388608 | tf_op jit(solution)/shard_map/pallas_call | solution.py:422
  45.3 0.0 copy-start
  45.3 0.0 copy-start.1
  45.3 3.1 %copy.13 = f32[4,32,32,128]{3,2,1,0:T(8,128)} copy(f32[4,32,32,128]{3,2,1,0:T(8,128)} %bitcast.6) | data formatting | bytes 4194304
  48.4 0.0 copy-done
  48.4 0.6 %copy.14 = f32[128,128]{1,0:T(8,128)} copy(f32[128,128]{1,0:T(8,128)S(1)} %copy-done) | data formatting | bytes 131072
  49.1 0.0 copy-done.1
  49.1 0.5 %copy.15 = s32[32]{0:T(128)} copy(s32[32]{0:T(128)S(1)} %bitcast.9) | data formatting | bytes 256
Async XLA Ops:
  45.3 3.1 %copy-start = (f32[128,128]{1,0:T(8,128)S(1)}, f32[128,128]{1,0:T(8,128)}, u32[]{:S(2)}) copy-start(f32[128,128]{1,0:T(8,128)} %get-tuple-element.13) | copy-start | bytes 196612
  45.3 3.8 %copy-start.1 = (s32[1,32]{1,0:T(1,128)S(1)}, s32[1,32]{1,0:T(1,128)}, u32[]{:S(2)}) copy-start(s32[1,32]{1,0:T(1,128)} %get-tuple-element.8) | copy-start | bytes 388

commit v2 on v1

v2 whole, which is shorter than its diff:
```python
import functools

import jax
import jax.numpy as jnp
from jax import lax
from jax.experimental import pallas as pl
from jax.experimental.pallas import tpu as pltpu
from jax.sharding import PartitionSpec as P

CAP = 4
BOX = 8
PADR = 8
MESH = pl.DeviceIdType.MESH


def kernel(
    dims, area_h, cell_h, owner_h, mask_h, east_h, north_h, tracers_h, final, arrivals, counts,
    area, cell, owner, mask, east, north, first, second, wet, flow, coef,
    cols, send_l, send_r, get_l, get_r, send_n, send_s, get_n, get_s,
    pick, halves, taken, outbox, inbox,
    in_sem, halo_send, halo_recv, box_send, box_recv,
):
    tracer_count, levels, rows, n_lat, n_lon = dims
    planes = tracer_count * levels
    tall = rows + 2 * PADR
    n_dev = n_lat * n_lon
    slots = n_dev * BOX
    floats = cell.shape[1]
    lat, lon = lax.axis_index("lat"), lax.axis_index("lon")
    me = lat * n_lon + lon
    top = lat == n_lat - 1
    bottom = lat == 0

    loads = [
        pltpu.make_async_copy(mask_h, mask, in_sem.at[0]),
        pltpu.make_async_copy(east_h, east, in_sem.at[1]),
        pltpu.make_async_copy(north_h, north, in_sem.at[2]),
        pltpu.make_async_copy(tracers_h, first.at[:, pl.ds(PADR, rows), :], in_sem.at[3]),
        pltpu.make_async_copy(area_h, area, in_sem.at[4]),
        pltpu.make_async_copy(cell_h, cell, in_sem.at[5]),
        pltpu.make_async_copy(owner_h, owner, in_sem.at[6]),
    ]
    for load in loads:
        load.start()

    barrier = pltpu.get_barrier_semaphore()

    def greet(j, carry):
        other = lax.rem(me + j, n_dev)
        pl.semaphore_signal(
            barrier, inc=1, device_id=(other // n_lon, lax.rem(other, n_lon)), device_id_type=MESH
        )
        return carry

    lax.fori_loop(1, n_dev, greet, 0)

    lane = lax.broadcasted_iota(jnp.int32, (8, 128), 1)
    group = lane // 4
    low_pair = lax.rem(lane, 4) < 2
    groups = rows // 8

    inner, outer = tuple(range(1, groups - 1)), (0, groups - 1)
    parts = (inner, outer)
    pairs = tracer_count // 2
    first_flat = first.reshape(planes * tall, 128)
    second_flat = second.reshape(planes * tall, 128)
    wet_flat = wet.reshape(levels * tall, 128)
    flow_flat = flow.reshape(levels * tall, 128)
    blank = jnp.zeros((8, 128), jnp.float32)

    for load in loads[:4]:
        load.wait()

    def gather_columns(k, acc):
        acc = list(acc)
        here = group == k
        for g in range(groups):
            at = pl.ds(PADR + 8 * g, 8)
            sub = pl.ds(8 * g, 8)
            water = mask[k, sub, :].astype(jnp.float32)
            wet[k, at, :] = water
            flow[k, at, :] = north[k, sub, :] * water
            edge = jnp.where(lane == 0, water, east[k, sub, :] * water)
            values = [first[c * levels + k, at, :] for c in range(tracer_count)] + [edge]
            for c, value in enumerate(values):
                i = g * (tracer_count + 1) + c
                acc[i] = jnp.where(here, pltpu.roll(value, 4 * k + 2, 1), acc[i])
        return tuple(acc)

    def fill_columns(packed, step, part):
        per = len(packed) // len(parts[part])
        for n in range(len(parts[part])):
            mine = packed[n * per : (n + 1) * per]
            for pair in range(pairs):
                a, b = mine[2 * pair], mine[2 * pair + 1]
                sub = pl.ds(pair * 8 * len(parts[part]) + 8 * n, 8)
                send_r[step, part, sub, :] = jnp.where(low_pair, a, pltpu.roll(b, 2, 1))
                send_l[step, part, sub, :] = jnp.where(low_pair, pltpu.roll(b, 126, 1), a)
            if step == 0:
                sub = pl.ds(pairs * 8 * len(parts[part]) + 8 * n, 8)
                send_r[step, part, sub, :] = mine[tracer_count]
                send_l[step, part, sub, :] = mine[tracer_count]

    def place_columns(step, part):
        for n, g in enumerate(parts[part]):
            at = pl.ds(8 * g, 8)
            for pair in range(pairs):
                sub = pl.ds(pair * 8 * len(parts[part]) + 8 * n, 8)
                from_l, from_r = get_l[step, part, sub, :], get_r[step, part, sub, :]
                cols[2 * pair, at, :] = jnp.where(low_pair, from_l, from_r)
                cols[2 * pair + 1, at, :] = jnp.where(
                    low_pair, pltpu.roll(from_l, 126, 1), pltpu.roll(from_r, 2, 1)
                )
            if step == 0:
                sub = pl.ds(pairs * 8 * len(parts[part]) + 8 * n, 8)
                cols[tracer_count, at, :] = jnp.where(
                    low_pair, get_l[step, part, sub, :], get_r[step, part, sub, :]
                )

    def fill_rows(flat, step):
        def row(r):
            return flat[pl.ds(PADR + r, planes, stride=tall), :]

        def water(r):
            line = mask.reshape(levels * rows, 128)[pl.ds(r, levels, stride=rows), :]
            return line.astype(jnp.float32)

        def stream(r):
            return north.reshape(levels * rows, 128)[pl.ds(r, levels, stride=rows), :] * water(r)

        @pl.when(jnp.logical_not(top))
        def _():
            send_n[step, pl.ds(0, planes), :] = row(rows - 2)
            send_n[step, pl.ds(planes, planes), :] = row(rows - 1)
            if step == 0:
                send_n[step, pl.ds(2 * planes, levels), :] = stream(rows - 1)

        @pl.when(top)
        def _():
            ahead = lax.broadcasted_iota(jnp.int32, (128, 128), 0)
            across = lax.broadcasted_iota(jnp.int32, (128, 128), 1)
            turn = (ahead + across == 127).astype(jnp.float32)

            def turned(value):
                return jnp.dot(
                    value, turn, precision=lax.Precision.HIGHEST, preferred_element_type=jnp.float32
                )

            send_n[step, pl.ds(0, planes), :] = turned(row(rows - 1))
            send_n[step, pl.ds(planes, planes), :] = turned(row(rows - 2))
            if step == 0:
                send_n[step, pl.ds(2 * planes, levels), :] = turned(water(rows - 1))

        send_s[step, pl.ds(0, planes), :] = row(0)
        send_s[step, pl.ds(planes, planes), :] = row(1)
        if step == 0:
            send_s[step, pl.ds(2 * planes, levels), :] = water(0)

    right, left = lax.rem(lon + 1, n_lon), lax.rem(lon + n_lon - 1, n_lon)
    upper = (jnp.where(top, lat, lat + 1), jnp.where(top, n_lon - 1 - lon, lon))
    lower = (jnp.where(bottom, 0, lat - 1), lon)

    def column_copies(step, part):
        size = (pairs + (1 if step == 0 else 0)) * 8 * len(parts[part])
        return [
            pltpu.make_async_remote_copy(
                src_ref=source.at[step, part, pl.ds(0, size)],
                dst_ref=target.at[step, part, pl.ds(0, size)],
                send_sem=halo_send.at[step, 2 * part + i],
                recv_sem=halo_recv.at[step, 2 * part + i],
                device_id=(lat, device),
                device_id_type=MESH,
            )
            for i, (source, target, device) in enumerate(
                ((send_r, get_l, right), (send_l, get_r, left))
            )
        ]

    def start_columns(step, part):
        for copy in column_copies(step, part):
            copy.start()

    def wait_columns(step, part):
        for copy in column_copies(step, part):
            copy.wait()

    def row_copy(step, source, target, out, come, device):
        size = 2 * planes + (levels if step == 0 else 0)
        return pltpu.make_async_remote_copy(
            src_ref=source.at[step, pl.ds(0, size)],
            dst_ref=target.at[step, pl.ds(0, size)],
            send_sem=halo_send.at[step, out],
            recv_sem=halo_recv.at[step, come],
            device_id=device,
            device_id_type=MESH,
        )

    def up_copy(step):
        return row_copy(step, send_n, get_s, 4, 4, upper)

    def down_copy(step):
        return row_copy(step, send_s, get_n, 5, 5, lower)

    def fold_copy(step):
        return row_copy(step, send_n, get_n, 4, 5, upper)

    def start_rows(step):
        @pl.when(top)
        def _():
            fold_copy(step).start()

        @pl.when(jnp.logical_not(top))
        def _():
            up_copy(step).start()

        @pl.when(jnp.logical_not(bottom))
        def _():
            down_copy(step).start()

    def wait_rows(step):
        up_copy(step).wait_send()
        down_copy(step).wait_recv()

        @pl.when(jnp.logical_not(bottom))
        def _():
            down_copy(step).wait_send()
            up_copy(step).wait_recv()

    def place_rows(flat, step):
        for i in range(2):
            flat[pl.ds(PADR + rows + i, planes, stride=tall), :] = get_n[
                step, pl.ds(i * planes, planes), :
            ]
        if step == 0:
            wet_flat[pl.ds(PADR + rows, levels, stride=tall), :] = get_n[
                step, pl.ds(2 * planes, levels), :
            ]

        @pl.when(bottom)
        def _():
            for i in range(2):
                flat[pl.ds(PADR - 2 + i, planes, stride=tall), :] = jnp.zeros((planes, 128), jnp.float32)
            if step == 0:
                flow_flat[pl.ds(PADR - 1, levels, stride=tall), :] = jnp.zeros((levels, 128), jnp.float32)

        @pl.when(jnp.logical_not(bottom))
        def _():
            for i in range(2):
                flat[pl.ds(PADR - 2 + i, planes, stride=tall), :] = get_s[
                    step, pl.ds(i * planes, planes), :
                ]
            if step == 0:
                flow_flat[pl.ds(PADR - 1, levels, stride=tall), :] = get_s[
                    step, pl.ds(2 * planes, levels), :
                ]

    def make_coefficients(k, g):
        at = pl.ds(PADR + 8 * g, 8)
        sub = pl.ds(8 * g, 8)
        beside = pltpu.roll(cols[tracer_count, sub, :], 126 - 4 * k, 1)
        water = wet[k, at, :]
        scale = area[sub, :] * water * (1.0 / 6.0)
        stream = east[k, sub, :] * water
        face_e = stream * pltpu.roll(jnp.where(lane == 0, beside, water), 127, 1)
        face_w = pltpu.roll(jnp.where(lane == 127, beside, stream), 1, 1) * water
        line = k * tall + PADR + 8 * g
        face_n = flow[k, at, :] * wet_flat[pl.ds(line + 1, 8), :]
        face_s = flow_flat[pl.ds(line - 1, 8), :] * water
        made = []
        centre = 1.0
        for ahead, behind in ((face_e, face_w), (face_n, face_s)):
            pos, neg = jnp.maximum(ahead, 0.0) * scale, jnp.minimum(ahead, 0.0) * scale
            pos_b, neg_b = jnp.maximum(behind, 0.0) * scale, jnp.minimum(behind, 0.0) * scale
            centre = centre - (5.0 * (pos - neg_b) + 2.0 * (neg - pos_b))
            made += [
                -pos_b,
                pos + 5.0 * pos_b + 2.0 * neg_b,
                -(2.0 * pos + 5.0 * neg + neg_b),
                neg,
            ]
        return [centre] + made

    def apply(flat, k, g, c, weights):
        centre, xm2, xm1, xp1, xp2, ym2, ym1, yp1, yp2 = weights
        base = (c * levels + k) * tall + PADR + 8 * g
        value = flat[pl.ds(pl.multiple_of(base, 8), 8), :]
        beside = pltpu.roll(cols[c, pl.ds(8 * g, 8), :], 126 - 4 * k, 1)
        total = centre * value
        total += xm2 * pltpu.roll(jnp.where(lane >= 126, beside, value), 2, 1)
        total += xm1 * pltpu.roll(jnp.where(lane == 127, beside, value), 1, 1)
        total += xp1 * pltpu.roll(jnp.where(lane == 0, beside, value), 127, 1)
        total += xp2 * pltpu.roll(jnp.where(lane <= 1, beside, value), 126, 1)
        total += ym2 * flat[pl.ds(base - 2, 8), :]
        total += ym1 * flat[pl.ds(base - 1, 8), :]
        total += yp1 * flat[pl.ds(base + 1, 8), :]
        total += yp2 * flat[pl.ds(base + 2, 8), :]
        return total

    def first_step(part):
        def level(k, acc):
            acc = list(acc)
            here = group == k
            for n, g in enumerate(parts[part]):
                weights = make_coefficients(k, g)
                for w, weight in enumerate(weights):
                    coef[k, w, pl.ds(8 * g, 8), :] = weight
                for c in range(tracer_count):
                    value = apply(first_flat, k, g, c, weights)
                    second[c * levels + k, pl.ds(PADR + 8 * g, 8), :] = value
                    i = n * tracer_count + c
                    acc[i] = jnp.where(here, pltpu.roll(value, 4 * k + 2, 1), acc[i])
            return tuple(acc)

        start = (blank,) * (tracer_count * len(parts[part]))
        return lax.fori_loop(0, levels, level, start, unroll=2)

    def second_step(part):
        def level(k, carry):
            for g in parts[part]:
                weights = [coef[k, w, pl.ds(8 * g, 8), :] for w in range(9)]
                for c in range(tracer_count):
                    final[c * levels + k, pl.ds(8 * g, 8), :] = apply(second_flat, k, g, c, weights)
            return carry

        lax.fori_loop(0, levels, level, 0, unroll=2)

    fill_rows(first_flat, 0)
    pl.semaphore_wait(barrier, n_dev - 1)
    start_rows(0)
    packed = lax.fori_loop(0, levels, gather_columns, (blank,) * ((tracer_count + 1) * groups), unroll=2)
    packed = [packed[g * (tracer_count + 1) : (g + 1) * (tracer_count + 1)] for g in range(groups)]
    for part in range(2):
        fill_columns(sum([packed[g] for g in parts[part]], ()), 0, part)
        start_columns(0, part)

    for load in loads[4:]:
        load.wait()
    cell_row, owner_row = cell[...], owner[...]
    f_row = lax.broadcasted_iota(jnp.int32, (floats, floats), 0)
    f_col = lax.broadcasted_iota(jnp.int32, (floats, floats), 1)
    diagonal = f_row == f_col
    owner_f = owner_row.astype(jnp.float32)
    owner_col = jnp.sum(jnp.where(diagonal, owner_f, 0.0), axis=1, keepdims=True)
    cell_col = jnp.sum(jnp.where(diagonal, cell_row.astype(jnp.float32), 0.0), axis=1, keepdims=True)
    rank = jnp.sum(
        jnp.where((owner_col == owner_f) & (f_col < f_row), 1.0, 0.0), axis=1, keepdims=True
    )
    slot_col = owner_col * float(BOX) + rank
    slot_lane = lax.broadcasted_iota(jnp.int32, (floats, slots), 1).astype(jnp.float32)
    wanted = jnp.sum(jnp.where(slot_col == slot_lane, cell_col + 1.0, 0.0), axis=0, keepdims=True) - 1.0
    wanted = wanted.astype(jnp.int32)
    slot_row = lax.broadcasted_iota(jnp.int32, (slots, floats), 0)
    tally = jnp.sum(
        jnp.where(owner_row * BOX + CAP == slot_row, 1.0, 0.0), axis=1, keepdims=True
    )

    def mark(r, carry):
        start = pl.multiple_of(r * 128, 128)
        place = lax.broadcasted_iota(jnp.int32, (128, slots), 0) + start
        pick[pl.ds(start, 128), :] = jnp.where(place == wanted, 1.0, 0.0).astype(jnp.bfloat16)
        return carry

    lax.fori_loop(0, rows, mark, 0)

    wait_columns(0, 0)
    place_columns(0, 0)
    packed = first_step(0)
    fill_columns(packed, 1, 0)
    start_columns(1, 0)
    wait_rows(0)
    place_rows(first_flat, 0)
    wait_columns(0, 1)
    place_columns(0, 1)
    packed = first_step(1)
    fill_rows(second_flat, 1)
    start_rows(1)
    fill_columns(packed, 1, 1)
    start_columns(1, 1)

    flat = final.reshape(planes * rows, 128)

    def take(low, high):
        for r in range(low, high):
            value = flat[pl.ds(r, planes, stride=rows), :]
            upper_half = value.astype(jnp.bfloat16)
            rest = (value - upper_half.astype(jnp.float32)).astype(jnp.bfloat16)
            halves[pl.ds(0, planes), pl.ds(r * 128, 128)] = upper_half
            halves[pl.ds(planes, planes), pl.ds(r * 128, 128)] = rest
        span = pl.ds(low * 128, (high - low) * 128)
        return jnp.dot(halves[:, span], pick[span, :], preferred_element_type=jnp.float32)

    wait_columns(1, 0)
    place_columns(1, 0)
    second_step(0)
    taken[...] = take(8, rows - 8)
    wait_rows(1)
    place_rows(second_flat, 1)
    wait_columns(1, 1)
    place_columns(1, 1)
    second_step(1)
    both = taken[...] + take(0, 8) + take(rows - 8, rows)
    outbox[...] = jnp.transpose(both[:planes] + both[planes:]) + tally

    def box_copy(j):
        other = lax.rem(me + j, n_dev)
        return pltpu.make_async_remote_copy(
            src_ref=outbox.at[pl.ds(pl.multiple_of(other * BOX, BOX), BOX)],
            dst_ref=inbox.at[pl.ds(pl.multiple_of(me * BOX, BOX), BOX)],
            send_sem=box_send.at[other],
            recv_sem=box_recv.at[me],
            device_id=(other // n_lon, lax.rem(other, n_lon)),
            device_id_type=MESH,
        )

    def box_start(j, carry):
        box_copy(j).start()
        return carry

    def box_wait(j, carry):
        other = lax.rem(me + j, n_dev)
        at = pl.ds(pl.multiple_of(other * BOX, BOX), BOX)
        copy = pltpu.make_async_remote_copy(
            src_ref=outbox.at[at],
            dst_ref=inbox.at[at],
            send_sem=box_send.at[other],
            recv_sem=box_recv.at[other],
            device_id=(other // n_lon, lax.rem(other, n_lon)),
            device_id_type=MESH,
        )
        copy.wait()
        return carry

    lax.fori_loop(1, n_dev, box_start, 0)
    own = pl.ds(pl.multiple_of(me * BOX, BOX), BOX)
    inbox[own, :] = outbox[own, :]
    lax.fori_loop(1, n_dev, box_wait, 0)
    for i in range(CAP):
        arrivals[pl.ds(i, n_dev, stride=CAP), :] = inbox[pl.ds(i, n_dev, stride=BOX), :]
    told = inbox[pl.ds(CAP, n_dev, stride=BOX), :][:, :n_dev]
    straight = lax.broadcasted_iota(jnp.int32, (n_dev, n_dev), 0) == lax.broadcasted_iota(
        jnp.int32, (n_dev, n_dev), 1
    )
    counts[...] = jnp.sum(jnp.where(straight, told, 0.0), axis=0, keepdims=True).astype(jnp.int32)


def local(tracers, vel_east, vel_north, land_mask, step_area, float_cell, float_owner):
    tracer_count, levels, rows, columns = tracers.shape
    n_lat, n_lon = lax.axis_size("lat"), lax.axis_size("lon")
    n_dev = n_lat * n_lon
    planes = tracer_count * levels
    tall = rows + 2 * PADR
    floats = float_cell.shape[0]
    row_size = 2 * planes + levels
    col_size = (tracer_count // 2 + 1) * max(rows - 16, 16)
    f32 = jnp.float32
    whole = pl.BlockSpec(memory_space=pl.ANY)
    vmem = pl.BlockSpec(memory_space=pltpu.VMEM)
    out, arrivals, counts = pl.pallas_call(
        functools.partial(kernel, (tracer_count, levels, rows, n_lat, n_lon)),
        out_shape=(
            pltpu.VMEM((planes, rows, columns), f32),
            pltpu.VMEM((n_dev * CAP, planes), f32),
            pltpu.VMEM((1, n_dev), jnp.int32),
        ),
        in_specs=[whole] * 7,
        out_specs=[vmem] * 3,
        scratch_shapes=[
            pltpu.VMEM((rows, columns), f32),
            pltpu.VMEM((1, floats), jnp.int32),
            pltpu.VMEM((1, floats), jnp.int32),
            pltpu.VMEM((levels, rows, columns), jnp.int32),
            pltpu.VMEM((levels, rows, columns), f32),
            pltpu.VMEM((levels, rows, columns), f32),
            pltpu.VMEM((planes, tall, columns), f32),
            pltpu.VMEM((planes, tall, columns), f32),
            pltpu.VMEM((levels, tall, columns), f32),
            pltpu.VMEM((levels, tall, columns), f32),
            pltpu.VMEM((levels, 9, rows, columns), f32),
            pltpu.VMEM((tracer_count + 1, rows, columns), f32),
            *[pltpu.VMEM((2, 2, col_size, columns), f32)] * 4,
            *[pltpu.VMEM((2, row_size, columns), f32)] * 4,
            pltpu.VMEM((rows * columns, n_dev * BOX), jnp.bfloat16),
            pltpu.VMEM((2 * planes, rows * columns), jnp.bfloat16),
            pltpu.VMEM((2 * planes, n_dev * BOX), f32),
            pltpu.VMEM((n_dev * BOX, planes), f32),
            pltpu.VMEM((n_dev * BOX, planes), f32),
            pltpu.SemaphoreType.DMA((7,)),
            pltpu.SemaphoreType.DMA((2, 6)),
            pltpu.SemaphoreType.DMA((2, 6)),
            pltpu.SemaphoreType.DMA((n_dev,)),
            pltpu.SemaphoreType.DMA((n_dev,)),
        ],
        compiler_params=pltpu.CompilerParams(
            collective_id=0, has_side_effects=True, vmem_limit_bytes=56 * 1024 * 1024
        ),
        cost_estimate=pl.CostEstimate(
            flops=2 * 17 * planes * rows * columns, bytes_accessed=8 * 1024 * 1024, transcendentals=0
        ),
    )(
        step_area,
        float_cell.reshape(1, floats),
        float_owner.reshape(1, floats),
        land_mask,
        vel_east,
        vel_north,
        tracers.reshape(planes, rows, columns),
    )
    return out.reshape(tracers.shape), arrivals, counts.reshape(n_dev)


def solution(mesh):
    placed = (
        P(None, None, "lat", "lon"),
        P(None, "lat", "lon"),
        P(None, "lat", "lon"),
        P(None, "lat", "lon"),
        P("lat", "lon"),
        P(("lat", "lon")),
        P(("lat", "lon"), None),
    )
    return jax.shard_map(
        local,
        mesh=mesh,
        in_specs=placed,
        out_specs=(P(None, None, "lat", "lon"), P(("lat", "lon"), None), P(("lat", "lon"))),
        check_vma=False,
    )
```

time: 49.7 us -> 41.3 us (0.83)
  Pallas kernels: 44.7 us -> 38 us
  local copies, waits for them, and re-layouts: 4.26 us -> 2.46 us
    pallas_call x1, Pallas kernels: 44.7 us -> 38 us  [local(): pl.pallas_call(functools.partial(kernel, (tracer_count, levels, rows, n_l...]
    unnamed x7 -> x3, local copies, waits for them, and re-layouts: 4.26 us -> 2.46 us
where the time goes in v2:
time: 41.3 us; the launch traced here: 41.1 us
  Pallas kernels  38 us (92%)
  local copies, waits for them, and re-layouts  2.46 us (6%)
  between operations  0.64 us (2%)
    pallas_call x1, Pallas kernels, local(): pl.pallas_call(functools.partial(kernel, (tracer_count, levels, rows, n_l...  38 us
    unnamed x3, local copies, waits for them, and re-layouts  2.46 us

profile of v2, /device:TPU:0, one launch (start us, length us, event | category | flops | bytes accessed | tf_op | source)
XLA Modules:
  0.0 41.1 jit_solution(17200180123079565701)
XLA Ops:
  0.6 38.0 %shard_map.94 = (f32[128,32,128]{2,1,0:T(8,128)S(1)}, f32[128,128]{1,0:T(8,128)S(1)}, s32[1,32]{1,0:T(1,128)S(1)}) custom-call(f32[32,128]{1,0:T(8,128)} %area_h.1, s32[1,64]{1,0:T(1,128)} %bitcast.8, s32[1,64]{1,0:T(1,128)} %bitcast.9, s32[32,32,128]{2,1,0:T(8,128)} %mask_h.1, f32[32,32,128]{2,1,0:T(8,128)} %east_h.1, f32[32,32,128]{2,1,0:T(8,128)} %north_h.1, ...), custom_call_target="tpu_custom_call" | custom-call | flops 17825792 | bytes 8388608 | tf_op jit(solution)/shard_map/pallas_call | solution.py:458
  38.7 1.3 %copy.13 = f32[4,32,32,128]{3,2,1,0:T(8,128)} copy(f32[4,32,32,128]{3,2,1,0:T(8,128)S(1)} %bitcast.5) | data formatting | bytes 4194304
  40.0 0.5 %copy.15 = s32[32]{0:T(128)} copy(s32[32]{0:T(128)S(1)} %bitcast.6) | data formatting | bytes 256
  40.5 0.6 %copy.14 = f32[128,128]{1,0:T(8,128)} copy(f32[128,128]{1,0:T(8,128)S(1)} %get-tuple-element.10) | data formatting | bytes 131072

commit v3 on v2

--- a/solution.py
+++ b/solution.py
@@ -45,14 +45,14 @@
 
     barrier = pltpu.get_barrier_semaphore()
 
-    def greet(j, carry):
-        other = lax.rem(me + j, n_dev)
-        pl.semaphore_signal(
-            barrier, inc=1, device_id=(other // n_lon, lax.rem(other, n_lon)), device_id_type=MESH
-        )
-        return carry
-
-    lax.fori_loop(1, n_dev, greet, 0)
+    def wrapped(at, step, size):
+        return jnp.where(at + step >= size, at + step - size, at + step)
+
+    lats = [wrapped(lat, i, n_lat) for i in range(n_lat)]
+    lons = [wrapped(lon, i, n_lon) for i in range(n_lon)]
+    others = [(a, b) for a in lats for b in lons][1:]
+    for other in others:
+        pl.semaphore_signal(barrier, inc=1, device_id=other, device_id_type=MESH)
 
     lane = lax.broadcasted_iota(jnp.int32, (8, 128), 1)
     group = lane // 4
@@ -312,7 +312,7 @@
             return tuple(acc)
 
         start = (blank,) * (tracer_count * len(parts[part]))
-        return lax.fori_loop(0, levels, level, start, unroll=2)
+        return lax.fori_loop(0, levels, level, start, unroll=4)
 
     def second_step(part):
         def level(k, carry):
@@ -322,12 +322,12 @@
                     final[c * levels + k, pl.ds(8 * g, 8), :] = apply(second_flat, k, g, c, weights)
             return carry
 
-        lax.fori_loop(0, levels, level, 0, unroll=2)
+        lax.fori_loop(0, levels, level, 0, unroll=4)
 
     fill_rows(first_flat, 0)
     pl.semaphore_wait(barrier, n_dev - 1)
     start_rows(0)
-    packed = lax.fori_loop(0, levels, gather_columns, (blank,) * ((tracer_count + 1) * groups), unroll=2)
+    packed = lax.fori_loop(0, levels, gather_columns, (blank,) * ((tracer_count + 1) * groups), unroll=4)
     packed = [packed[g * (tracer_count + 1) : (g + 1) * (tracer_count + 1)] for g in range(groups)]
     for part in range(2):
         fill_columns(sum([packed[g] for g in parts[part]], ()), 0, part)
@@ -360,7 +360,7 @@
         pick[pl.ds(start, 128), :] = jnp.where(place == wanted, 1.0, 0.0).astype(jnp.bfloat16)
         return carry
 
-    lax.fori_loop(0, rows, mark, 0)
+    lax.fori_loop(0, rows, mark, 0, unroll=2)
 
     wait_columns(0, 0)
     place_columns(0, 0)
@@ -401,39 +401,25 @@
     both = taken[...] + take(0, 8) + take(rows - 8, rows)
     outbox[...] = jnp.transpose(both[:planes] + both[planes:]) + tally
 
-    def box_copy(j):
-        other = lax.rem(me + j, n_dev)
+    own = pl.ds(pl.multiple_of(me * BOX, BOX), BOX)
+
+    def box_copy(other, come):
+        number = other[0] * n_lon + other[1]
+        at = pl.ds(pl.multiple_of(number * BOX, BOX), BOX)
         return pltpu.make_async_remote_copy(
-            src_ref=outbox.at[pl.ds(pl.multiple_of(other * BOX, BOX), BOX)],
-            dst_ref=inbox.at[pl.ds(pl.multiple_of(me * BOX, BOX), BOX)],
-            send_sem=box_send.at[other],
-            recv_sem=box_recv.at[me],
-            device_id=(other // n_lon, lax.rem(other, n_lon)),
+            src_ref=outbox.at[at],
+            dst_ref=inbox.at[at if come else own],
+            send_sem=box_send.at[number],
+            recv_sem=box_recv.at[number if come else me],
+            device_id=other,
             device_id_type=MESH,
         )
 
-    def box_start(j, carry):
-        box_copy(j).start()
-        return carry
-
-    def box_wait(j, carry):
-        other = lax.rem(me + j, n_dev)
-        at = pl.ds(pl.multiple_of(other * BOX, BOX), BOX)
-        copy = pltpu.make_async_remote_copy(
-            src_ref=outbox.at[at],
-            dst_ref=inbox.at[at],
-            send_sem=box_send.at[other],
-            recv_sem=box_recv.at[other],
-            device_id=(other // n_lon, lax.rem(other, n_lon)),
-            device_id_type=MESH,
-        )
-        copy.wait()
-        return carry
-
-    lax.fori_loop(1, n_dev, box_start, 0)
-    own = pl.ds(pl.multiple_of(me * BOX, BOX), BOX)
+    for other in others:
+        box_copy(other, False).start()
     inbox[own, :] = outbox[own, :]
-    lax.fori_loop(1, n_dev, box_wait, 0)
+    for other in others:
+        box_copy(other, True).wait()
     for i in range(CAP):
         arrivals[pl.ds(i, n_dev, stride=CAP), :] = inbox[pl.ds(i, n_dev, stride=BOX), :]
     told = inbox[pl.ds(CAP, n_dev, stride=BOX), :][:, :n_dev]

time: 41.3 us -> 46.9 us (1.14)
  Pallas kernels: 38 us -> 43.6 us
    pallas_call x1, Pallas kernels: 38 us -> 43.6 us  [local(): pl.pallas_call(functools.partial(kernel, (tracer_count, levels, rows, n_l...]
where the time goes in v3:
time: 46.9 us; the launch traced here: 46.7 us
  Pallas kernels  43.6 us (93%)
  local copies, waits for them, and re-layouts  2.46 us (5%)
  between operations  0.64 us (1%)
    pallas_call x1, Pallas kernels, local(): pl.pallas_call(functools.partial(kernel, (tracer_count, levels, rows, n_l...  43.6 us
    unnamed x3, local copies, waits for them, and re-layouts  2.46 us

profile of v3, /device:TPU:0, one launch (start us, length us, event | category | flops | bytes accessed | tf_op | source)
XLA Modules:
  0.0 46.7 jit_solution(937245359459646044)
XLA Ops:
  0.6 43.6 %shard_map.94 = (f32[128,32,128]{2,1,0:T(8,128)S(1)}, f32[128,128]{1,0:T(8,128)S(1)}, s32[1,32]{1,0:T(1,128)S(1)}) custom-call(f32[32,128]{1,0:T(8,128)} %area_h.1, s32[1,64]{1,0:T(1,128)} %bitcast.8, s32[1,64]{1,0:T(1,128)} %bitcast.9, s32[32,32,128]{2,1,0:T(8,128)} %mask_h.1, f32[32,32,128]{2,1,0:T(8,128)} %east_h.1, f32[32,32,128]{2,1,0:T(8,128)} %north_h.1, ...), custom_call_target="tpu_custom_call" | custom-call | flops 17825792 | bytes 8388608 | tf_op jit(solution)/shard_map/pallas_call | solution.py:444
  44.3 1.3 %copy.13 = f32[4,32,32,128]{3,2,1,0:T(8,128)} copy(f32[4,32,32,128]{3,2,1,0:T(8,128)S(1)} %bitcast.5) | data formatting | bytes 4194304
  45.6 0.5 %copy.15 = s32[32]{0:T(128)} copy(s32[32]{0:T(128)S(1)} %bitcast.6) | data formatting | bytes 256
  46.1 0.6 %copy.14 = f32[128,128]{1,0:T(8,128)} copy(f32[128,128]{1,0:T(8,128)S(1)} %get-tuple-element.10) | data formatting | bytes 131072

commit v4 on v2

v4 whole, which is shorter than its diff:
```python
import functools

import jax
import jax.numpy as jnp
from jax import lax
from jax.experimental import pallas as pl
from jax.experimental.pallas import tpu as pltpu
from jax.sharding import PartitionSpec as P

CAP = 4
BOX = 8
PADR = 8
MESH = pl.DeviceIdType.MESH


def kernel(
    dims, area_h, cell_h, owner_h, mask_h, east_h, north_h, tracers_h, final, arrivals, counts,
    area, cell, owner, mask, east, north, field, wet, flow, coef,
    pack, cols, send_l, send_r, get_l, get_r, send_n, send_s, get_n, get_s,
    pick, taken, outbox, inbox,
    in_sem, out_sem, halo_send, halo_recv, box_send, box_recv,
):
    tracer_count, levels, rows, n_lat, n_lon = dims
    planes = tracer_count * levels
    tall = rows + 2 * PADR
    n_dev = n_lat * n_lon
    slots = n_dev * BOX
    floats = cell.shape[1]
    groups = rows // 8
    wide = groups // 2
    pairs = tracer_count // 2
    lat, lon = lax.axis_index("lat"), lax.axis_index("lon")
    me = lat * n_lon + lon
    top = lat == n_lat - 1
    bottom = lat == 0

    loads = [
        pltpu.make_async_copy(mask_h, mask, in_sem.at[0]),
        pltpu.make_async_copy(east_h, east, in_sem.at[1]),
        pltpu.make_async_copy(north_h, north, in_sem.at[2]),
        pltpu.make_async_copy(tracers_h, field.at[0, :, pl.ds(PADR, rows), :], in_sem.at[3]),
        pltpu.make_async_copy(area_h, area, in_sem.at[4]),
        pltpu.make_async_copy(cell_h, cell, in_sem.at[5]),
        pltpu.make_async_copy(owner_h, owner, in_sem.at[6]),
    ]
    for load in loads:
        load.start()

    barrier = pltpu.get_barrier_semaphore()

    def device(number):
        return (lax.div(number, n_lon), lax.rem(number, n_lon))

    def after_me(j):
        return jnp.where(me + j >= n_dev, me + j - n_dev, me + j)

    def greet(j, carry):
        pl.semaphore_signal(barrier, inc=1, device_id=device(after_me(j)), device_id_type=MESH)
        return carry

    lax.fori_loop(1, n_dev, greet, 0)

    lane = lax.broadcasted_iota(jnp.int32, (8, 128), 1)
    group = lane // 4
    low_pair = lax.rem(lane, 4) < 2
    flat = field.reshape(3 * planes * tall, 128)
    wet_flat = wet.reshape(levels * tall, 128)
    flow_flat = flow.reshape(levels * tall, 128)
    mask_flat = mask.reshape(levels * rows, 128)
    north_flat = north.reshape(levels * rows, 128)

    def group_of(part, n):
        if n < wide // 2:
            return n + jnp.where(part == 0, wide // 2, 0)
        return n + jnp.where(part == 0, wide // 2, wide)

    def eight(start):
        return pl.ds(pl.multiple_of(start, 8), 8)

    for load in loads:
        load.wait()

    def gather_columns(k, acc):
        acc = list(acc)
        here = group == k
        for g in range(groups):
            at = pl.ds(PADR + 8 * g, 8)
            sub = pl.ds(8 * g, 8)
            water = mask[k, sub, :].astype(jnp.float32)
            wet[k, at, :] = water
            flow[k, at, :] = north[k, sub, :] * water
            edge = jnp.where(lane == 0, water, east[k, sub, :] * water)
            values = [field[0, c * levels + k, at, :] for c in range(tracer_count)] + [edge]
            for c, value in enumerate(values):
                i = c * groups + g
                acc[i] = jnp.where(here, pltpu.roll(value, 4 * k + 2, 1), acc[i])
        return tuple(acc)

    right, left = lax.rem(lon + 1, n_lon), lax.rem(lon + n_lon - 1, n_lon)
    upper = (jnp.where(top, lat, lat + 1), jnp.where(top, n_lon - 1 - lon, lon))
    lower = (jnp.where(bottom, 0, lat - 1), lon)

    def column_copy(step, part, i):
        source, target, to = ((send_r, get_l, right), (send_l, get_r, left))[i]
        return pltpu.make_async_remote_copy(
            src_ref=source.at[step, part],
            dst_ref=target.at[step, part],
            send_sem=halo_send.at[step, 2 * part + i],
            recv_sem=halo_recv.at[step, 2 * part + i],
            device_id=(lat, to),
            device_id_type=MESH,
        )

    def send_columns(step, part):
        for n in range(wide):
            at = eight(8 * group_of(part, n))
            for pair in range(pairs):
                a, b = pack[2 * pair, at, :], pack[2 * pair + 1, at, :]
                sub = pl.ds((pair * wide + n) * 8, 8)
                send_r[step, part, sub, :] = jnp.where(low_pair, a, pltpu.roll(b, 2, 1))
                send_l[step, part, sub, :] = jnp.where(low_pair, pltpu.roll(b, 126, 1), a)
            sub = pl.ds((pairs * wide + n) * 8, 8)
            send_r[step, part, sub, :] = pack[tracer_count, at, :]
            send_l[step, part, sub, :] = pack[tracer_count, at, :]
        column_copy(step, part, 0).start()
        column_copy(step, part, 1).start()

    def take_columns(step, part):
        column_copy(step, part, 0).wait()
        column_copy(step, part, 1).wait()
        for n in range(wide):
            at = eight(8 * group_of(part, n))
            for pair in range(pairs):
                sub = pl.ds((pair * wide + n) * 8, 8)
                from_l, from_r = get_l[step, part, sub, :], get_r[step, part, sub, :]
                cols[2 * pair, at, :] = jnp.where(low_pair, from_l, from_r)
                cols[2 * pair + 1, at, :] = jnp.where(
                    low_pair, pltpu.roll(from_l, 126, 1), pltpu.roll(from_r, 2, 1)
                )
            sub = pl.ds((pairs * wide + n) * 8, 8)
            cols[tracer_count, at, :] = jnp.where(
                low_pair, get_l[step, part, sub, :], get_r[step, part, sub, :]
            )

    def row_copy(step, source, target, out, come, to):
        return pltpu.make_async_remote_copy(
            src_ref=source.at[step],
            dst_ref=target.at[step],
            send_sem=halo_send.at[step, out],
            recv_sem=halo_recv.at[step, come],
            device_id=to,
            device_id_type=MESH,
        )

    def up_copy(step):
        return row_copy(step, send_n, get_s, 4, 4, upper)

    def down_copy(step):
        return row_copy(step, send_s, get_n, 5, 5, lower)

    def fold_copy(step):
        return row_copy(step, send_n, get_n, 4, 5, upper)

    def send_rows(step):
        start = step * (planes * tall) + PADR

        def row(r):
            return flat[pl.ds(start + r, planes, stride=tall), :]

        send_s[step, pl.ds(0, planes), :] = row(0)
        send_s[step, pl.ds(planes, planes), :] = row(1)
        send_s[step, pl.ds(2 * planes, levels), :] = mask_flat[
            pl.ds(0, levels, stride=rows), :
        ].astype(jnp.float32)

        @pl.when(jnp.logical_not(bottom))
        def _():
            down_copy(step).start()

        last, before = row(rows - 1), row(rows - 2)
        edge = pl.ds(rows - 1, levels, stride=rows)
        water = mask_flat[edge, :].astype(jnp.float32)
        send_n[step, pl.ds(0, planes), :] = jnp.where(top, last, before)
        send_n[step, pl.ds(planes, planes), :] = jnp.where(top, before, last)
        send_n[step, pl.ds(2 * planes, levels), :] = water * jnp.where(top, 1.0, north_flat[edge, :])

        @pl.when(top)
        def _():
            ahead = lax.broadcasted_iota(jnp.int32, (128, 128), 0)
            across = lax.broadcasted_iota(jnp.int32, (128, 128), 1)
            turn = (ahead + across == 127).astype(jnp.float32)

            def reverse(i, carry):
                at = pl.ds(pl.multiple_of(i * levels, levels), levels)
                send_n[step, at, :] = jnp.dot(
                    send_n[step, at, :],
                    turn,
                    precision=lax.Precision.HIGHEST,
                    preferred_element_type=jnp.float32,
                )
                return carry

            lax.fori_loop(0, 2 * tracer_count + 1, reverse, 0)
            fold_copy(step).start()

        @pl.when(jnp.logical_not(top))
        def _():
            up_copy(step).start()

    def take_rows(step):
        up_copy(step).wait_send()
        down_copy(step).wait_recv()
        start = step * (planes * tall) + PADR
        for i in range(2):
            flat[pl.ds(start + rows + i, planes, stride=tall), :] = get_n[
                step, pl.ds(i * planes, planes), :
            ]
        wet_flat[pl.ds(PADR + rows, levels, stride=tall), :] = get_n[
            step, pl.ds(2 * planes, levels), :
        ]

        @pl.when(bottom)
        def _():
            get_s[step] = jnp.zeros((2 * planes + levels, 128), jnp.float32)

        @pl.when(jnp.logical_not(bottom))
        def _():
            down_copy(step).wait_send()
            up_copy(step).wait_recv()

        for i in range(2):
            flat[pl.ds(start - 2 + i, planes, stride=tall), :] = get_s[
                step, pl.ds(i * planes, planes), :
            ]
        flow_flat[pl.ds(PADR - 1, levels, stride=tall), :] = get_s[step, pl.ds(2 * planes, levels), :]

    def make_coefficients(k, g):
        at = eight(PADR + 8 * g)
        sub = eight(8 * g)
        line = k * tall + PADR + 8 * g
        beside = pltpu.roll(cols[tracer_count, sub, :], 126 - 4 * k, 1)
        water = wet[k, at, :]
        scale = area[sub, :] * water * (1.0 / 6.0)
        stream = east[k, sub, :] * water
        face_e = stream * pltpu.roll(jnp.where(lane == 0, beside, water), 127, 1)
        face_w = pltpu.roll(jnp.where(lane == 127, beside, stream), 1, 1) * water
        face_n = flow[k, at, :] * wet_flat[pl.ds(line + 1, 8), :]
        face_s = flow_flat[pl.ds(line - 1, 8), :] * water
        made = []
        centre = 1.0
        for ahead, behind in ((face_e, face_w), (face_n, face_s)):
            pos, neg = jnp.maximum(ahead, 0.0) * scale, jnp.minimum(ahead, 0.0) * scale
            pos_b, neg_b = jnp.maximum(behind, 0.0) * scale, jnp.minimum(behind, 0.0) * scale
            centre = centre - (5.0 * (pos - neg_b) + 2.0 * (neg - pos_b))
            made += [
                -pos_b,
                pos + 5.0 * pos_b + 2.0 * neg_b,
                -(2.0 * pos + 5.0 * neg + neg_b),
                neg,
            ]
        for w, weight in enumerate([centre] + made):
            coef[k, w, sub, :] = weight

    def apply(base, beside, weights):
        centre, xm2, xm1, xp1, xp2, ym2, ym1, yp1, yp2 = weights
        value = flat[eight(base), :]
        total = centre * value
        total += xm2 * pltpu.roll(jnp.where(lane >= 126, beside, value), 2, 1)
        total += xm1 * pltpu.roll(jnp.where(lane == 127, beside, value), 1, 1)
        total += xp1 * pltpu.roll(jnp.where(lane == 0, beside, value), 127, 1)
        total += xp2 * pltpu.roll(jnp.where(lane <= 1, beside, value), 126, 1)
        total += ym2 * flat[pl.ds(base - 2, 8), :]
        total += ym1 * flat[pl.ds(base - 1, 8), :]
        total += yp1 * flat[pl.ds(base + 1, 8), :]
        total += yp2 * flat[pl.ds(base + 2, 8), :]
        return total

    def run_part(step, part):
        @pl.when(step == 0)
        def _():
            def level(k, carry):
                for n in range(wide):
                    make_coefficients(k, group_of(part, n))
                return carry

            lax.fori_loop(0, levels, level, 0)

        def level(k, acc):
            acc = list(acc)
            here = group == k
            for n in range(wide):
                g = group_of(part, n)
                sub = eight(8 * g)
                weights = [coef[k, w, sub, :] for w in range(9)]
                for c in range(tracer_count):
                    base = (step * planes + c * levels + k) * tall + PADR + 8 * g
                    beside = pltpu.roll(cols[c, sub, :], 126 - 4 * k, 1)
                    value = apply(base, beside, weights)
                    flat[eight(base + planes * tall), :] = value
                    i = n * tracer_count + c
                    acc[i] = jnp.where(here, pltpu.roll(value, 4 * k + 2, 1), acc[i])
            return tuple(acc)

        packed = lax.fori_loop(0, levels, level, (blank,) * (tracer_count * wide))
        for n in range(wide):
            for c in range(tracer_count):
                pack[c, eight(8 * group_of(part, n)), :] = packed[n * tracer_count + c]

    def take_cells(part):
        def two_rows(i, carry):
            r = 2 * jnp.where(part == 0, rows // 8 + i, jnp.where(i < rows // 8, i, i + rows // 4))
            start = 2 * planes * tall + PADR + r
            value = jnp.concatenate(
                [flat[pl.ds(start + h, planes, stride=tall), :] for h in range(2)], axis=1
            )
            high = value.astype(jnp.bfloat16)
            rest = (value - high.astype(jnp.float32)).astype(jnp.bfloat16)
            chosen = pick[pl.ds(pl.multiple_of(r * 128, 256), 256), :]
            taken[...] += jnp.dot(
                jnp.concatenate([high, rest], axis=0), chosen, preferred_element_type=jnp.float32
            )
            return carry

        lax.fori_loop(0, rows // 4, two_rows, 0)

    blank = jnp.zeros((8, 128), jnp.float32)
    packed = lax.fori_loop(0, levels, gather_columns, (blank,) * ((tracer_count + 1) * groups))
    for i, value in enumerate(packed):
        pack[i // groups, pl.ds(8 * (i % groups), 8), :] = value
    pl.semaphore_wait(barrier, n_dev - 1)

    def first_columns(part, carry):
        send_columns(0, part)
        return carry

    lax.fori_loop(0, 2, first_columns, 0)

    def one_step(step, carry):
        send_rows(step)

        @pl.when(step == 0)
        def _():
            prepare()

        def one_part(part, carry):
            take_columns(step, part)

            @pl.when(part == 1)
            def _():
                take_rows(step)

            run_part(step, part)

            @pl.when(step == 0)
            def _():
                send_columns(1, part)

            @pl.when(step == 1)
            def _():
                take_cells(part)

            return carry

        lax.fori_loop(0, 2, one_part, 0)
        return carry

    f_row = lax.broadcasted_iota(jnp.int32, (floats, floats), 0)
    f_col = lax.broadcasted_iota(jnp.int32, (floats, floats), 1)
    owner_row = owner[...]

    def prepare():
        diagonal = f_row == f_col
        cell_f, owner_f = cell[...].astype(jnp.float32), owner_row.astype(jnp.float32)
        owner_col = jnp.sum(jnp.where(diagonal, owner_f, 0.0), axis=1, keepdims=True)
        cell_col = jnp.sum(jnp.where(diagonal, cell_f, 0.0), axis=1, keepdims=True)
        rank = jnp.sum(
            jnp.where((owner_col == owner_f) & (f_col < f_row), 1.0, 0.0), axis=1, keepdims=True
        )
        slot_col = owner_col * float(BOX) + rank
        slot_lane = lax.broadcasted_iota(jnp.int32, (floats, slots), 1).astype(jnp.float32)
        wanted = jnp.sum(jnp.where(slot_col == slot_lane, cell_col + 1.0, 0.0), axis=0, keepdims=True)
        wanted = wanted.astype(jnp.int32) - 1
        taken[...] = jnp.zeros_like(taken)

        def mark(r, carry):
            start = pl.multiple_of(r * 32, 32)
            place = lax.broadcasted_iota(jnp.int32, (32, slots), 0) + start
            pick[pl.ds(start, 32), :] = jnp.where(place == wanted, 1.0, 0.0).astype(jnp.bfloat16)
            return carry

        lax.fori_loop(0, rows * 4, mark, 0)

    lax.fori_loop(0, 2, one_step, 0)
    store = pltpu.make_async_copy(field.at[2, :, pl.ds(PADR, rows), :], final, out_sem.at[0])
    store.start()

    slot_row = lax.broadcasted_iota(jnp.int32, (slots, floats), 0)
    tally = jnp.sum(jnp.where(owner_row * BOX + CAP == slot_row, 1.0, 0.0), axis=1, keepdims=True)
    outbox[...] = jnp.transpose(taken[pl.ds(0, planes), :] + taken[pl.ds(planes, planes), :]) + tally
    own = pl.ds(pl.multiple_of(me * BOX, BOX), BOX)

    def box_copy(j, come):
        other = after_me(j)
        at = pl.ds(pl.multiple_of(other * BOX, BOX), BOX)
        return pltpu.make_async_remote_copy(
            src_ref=outbox.at[at],
            dst_ref=inbox.at[at if come else own],
            send_sem=box_send.at[other],
            recv_sem=box_recv.at[other if come else me],
            device_id=device(other),
            device_id_type=MESH,
        )

    def box_start(j, carry):
        box_copy(j, False).start()
        return carry

    def box_wait(j, carry):
        box_copy(j, True).wait()
        return carry

    lax.fori_loop(1, n_dev, box_start, 0)
    inbox[own, :] = outbox[own, :]
    lax.fori_loop(1, n_dev, box_wait, 0)
    for i in range(CAP):
        arrivals[pl.ds(i, n_dev, stride=CAP), :] = inbox[pl.ds(i, n_dev, stride=BOX), :]
    told = inbox[pl.ds(CAP, n_dev, stride=BOX), :][:, :n_dev]
    straight = lax.broadcasted_iota(jnp.int32, (n_dev, n_dev), 0) == lax.broadcasted_iota(
        jnp.int32, (n_dev, n_dev), 1
    )
    counts[...] = jnp.sum(jnp.where(straight, told, 0.0), axis=0, keepdims=True).astype(jnp.int32)
    store.wait()


def local(tracers, vel_east, vel_north, land_mask, step_area, float_cell, float_owner):
    tracer_count, levels, rows, columns = tracers.shape
    n_lat, n_lon = lax.axis_size("lat"), lax.axis_size("lon")
    n_dev = n_lat * n_lon
    planes = tracer_count * levels
    tall = rows + 2 * PADR
    floats = float_cell.shape[0]
    row_size = 2 * planes + levels
    col_size = (tracer_count // 2 + 1) * rows // 2
    f32 = jnp.float32
    whole = pl.BlockSpec(memory_space=pl.ANY)
    vmem = pl.BlockSpec(memory_space=pltpu.VMEM)
    out, arrivals, counts = pl.pallas_call(
        functools.partial(kernel, (tracer_count, levels, rows, n_lat, n_lon)),
        out_shape=(
            pltpu.VMEM((planes, rows, columns), f32),
            pltpu.VMEM((n_dev * CAP, planes), f32),
            pltpu.VMEM((1, n_dev), jnp.int32),
        ),
        in_specs=[whole] * 7,
        out_specs=[vmem] * 3,
        scratch_shapes=[
            pltpu.VMEM((rows, columns), f32),
            pltpu.VMEM((1, floats), jnp.int32),
            pltpu.VMEM((1, floats), jnp.int32),
            pltpu.VMEM((levels, rows, columns), jnp.int32),
            pltpu.VMEM((levels, rows, columns), f32),
            pltpu.VMEM((levels, rows, columns), f32),
            pltpu.VMEM((3, planes, tall, columns), f32),
            pltpu.VMEM((levels, tall, columns), f32),
            pltpu.VMEM((levels, tall, columns), f32),
            pltpu.VMEM((levels, 9, rows, columns), f32),
            *[pltpu.VMEM((tracer_count + 1, rows, columns), f32)] * 2,
            *[pltpu.VMEM((2, 2, col_size, columns), f32)] * 4,
            *[pltpu.VMEM((2, row_size, columns), f32)] * 4,
            pltpu.VMEM((rows * columns, n_dev * BOX), jnp.bfloat16),
            pltpu.VMEM((2 * planes, n_dev * BOX), f32),
            pltpu.VMEM((n_dev * BOX, planes), f32),
            pltpu.VMEM((n_dev * BOX, planes), f32),
            pltpu.SemaphoreType.DMA((7,)),
            pltpu.SemaphoreType.DMA((1,)),
            pltpu.SemaphoreType.DMA((2, 6)),
            pltpu.SemaphoreType.DMA((2, 6)),
            pltpu.SemaphoreType.DMA((n_dev,)),
            pltpu.SemaphoreType.DMA((n_dev,)),
        ],
        compiler_params=pltpu.CompilerParams(
            collective_id=0, has_side_effects=True, vmem_limit_bytes=56 * 1024 * 1024
        ),
        cost_estimate=pl.CostEstimate(
            flops=2 * 17 * planes * rows * columns, bytes_accessed=8 * 1024 * 1024, transcendentals=0
        ),
    )(
        step_area,
        float_cell.reshape(1, floats),
        float_owner.reshape(1, floats),
        land_mask,
        vel_east,
        vel_north,
        tracers.reshape(planes, rows, columns),
    )
    return out.reshape(tracers.shape), arrivals, counts.reshape(n_dev)


def solution(mesh):
    placed = (
        P(None, None, "lat", "lon"),
        P(None, "lat", "lon"),
        P(None, "lat", "lon"),
        P(None, "lat", "lon"),
        P("lat", "lon"),
        P(("lat", "lon")),
        P(("lat", "lon"), None),
    )
    return jax.shard_map(
        local,
        mesh=mesh,
        in_specs=placed,
        out_specs=(P(None, None, "lat", "lon"), P(("lat", "lon"), None), P(("lat", "lon"))),
        check_vma=False,
    )
```

time: 41.3 us -> 80.3 us (1.94)
  Pallas kernels: 38 us -> 77.1 us
    pallas_call x1, Pallas kernels: 38 us -> 77.1 us  [local(): pl.pallas_call(functools.partial(kernel, (tracer_count, levels, rows, n_l...]
where the time goes in v4:
time: 80.3 us; the launch traced here: 80.2 us
  Pallas kernels  77.1 us (96%)
  local copies, waits for them, and re-layouts  2.46 us (3%)
    pallas_call x1, Pallas kernels, local(): pl.pallas_call(functools.partial(kernel, (tracer_count, levels, rows, n_l...  77.1 us
    unnamed x3, local copies, waits for them, and re-layouts  2.46 us

profile of v4, /device:TPU:0, one launch (start us, length us, event | category | flops | bytes accessed | tf_op | source)
XLA Modules:
  0.0 80.2 jit_solution(14449449600618006204)
XLA Ops:
  0.6 77.1 %shard_map.94 = (f32[128,32,128]{2,1,0:T(8,128)S(1)}, f32[128,128]{1,0:T(8,128)S(1)}, s32[1,32]{1,0:T(1,128)S(1)}) custom-call(f32[32,128]{1,0:T(8,128)} %area_h.1, s32[1,64]{1,0:T(1,128)} %bitcast.8, s32[1,64]{1,0:T(1,128)} %bitcast.9, s32[32,32,128]{2,1,0:T(8,128)} %mask_h.1, f32[32,32,128]{2,1,0:T(8,128)} %east_h.1, f32[32,32,128]{2,1,0:T(8,128)} %north_h.1, ...), custom_call_target="tpu_custom_call" | custom-call | flops 17825792 | bytes 8388608 | tf_op jit(solution)/shard_map/pallas_call | solution.py:447
  77.7 1.3 %copy.13 = f32[4,32,32,128]{3,2,1,0:T(8,128)} copy(f32[4,32,32,128]{3,2,1,0:T(8,128)S(1)} %bitcast.5) | data formatting | bytes 4194304
  79.0 0.5 copy.15
  79.5 0.6 copy.14

commit v5 on v2

--- a/solution.py
+++ b/solution.py
@@ -128,12 +128,13 @@
         def stream(r):
             return north.reshape(levels * rows, 128)[pl.ds(r, levels, stride=rows), :] * water(r)
 
-        @pl.when(jnp.logical_not(top))
-        def _():
-            send_n[step, pl.ds(0, planes), :] = row(rows - 2)
-            send_n[step, pl.ds(planes, planes), :] = row(rows - 1)
-            if step == 0:
-                send_n[step, pl.ds(2 * planes, levels), :] = stream(rows - 1)
+        last, before = row(rows - 1), row(rows - 2)
+        send_n[step, pl.ds(0, planes), :] = jnp.where(top, last, before)
+        send_n[step, pl.ds(planes, planes), :] = jnp.where(top, before, last)
+        if step == 0:
+            send_n[step, pl.ds(2 * planes, levels), :] = jnp.where(
+                top, water(rows - 1), stream(rows - 1)
+            )
 
         @pl.when(top)
         def _():
@@ -141,15 +142,17 @@
             across = lax.broadcasted_iota(jnp.int32, (128, 128), 1)
             turn = (ahead + across == 127).astype(jnp.float32)
 
-            def turned(value):
-                return jnp.dot(
-                    value, turn, precision=lax.Precision.HIGHEST, preferred_element_type=jnp.float32
+            def reverse(i, carry):
+                at = pl.ds(pl.multiple_of(i * levels, levels), levels)
+                send_n[step, at, :] = jnp.dot(
+                    send_n[step, at, :],
+                    turn,
+                    precision=lax.Precision.HIGHEST,
+                    preferred_element_type=jnp.float32,
                 )
-
-            send_n[step, pl.ds(0, planes), :] = turned(row(rows - 1))
-            send_n[step, pl.ds(planes, planes), :] = turned(row(rows - 2))
-            if step == 0:
-                send_n[step, pl.ds(2 * planes, levels), :] = turned(water(rows - 1))
+                return carry
+
+            lax.fori_loop(0, 2 * tracer_count + (1 if step == 0 else 0), reverse, 0)
 
         send_s[step, pl.ds(0, planes), :] = row(0)
         send_s[step, pl.ds(planes, planes), :] = row(1)
@@ -254,10 +257,9 @@
                     step, pl.ds(2 * planes, levels), :
                 ]
 
-    def make_coefficients(k, g):
+    def make_coefficients(k, g, beside):
         at = pl.ds(PADR + 8 * g, 8)
         sub = pl.ds(8 * g, 8)
-        beside = pltpu.roll(cols[tracer_count, sub, :], 126 - 4 * k, 1)
         water = wet[k, at, :]
         scale = area[sub, :] * water * (1.0 / 6.0)
         stream = east[k, sub, :] * water
@@ -280,49 +282,68 @@
             ]
         return [centre] + made
 
-    def apply(flat, k, g, c, weights):
+    def sides_of(part, k, count):
+        shift = (126 - 4 * k) & 127
+        return tuple(
+            pltpu.roll(cols[c, pl.ds(8 * g, 8), :], shift, 1) for g in parts[part] for c in range(count)
+        )
+
+    def apply(flat, k, g, c, weights, beside):
         centre, xm2, xm1, xp1, xp2, ym2, ym1, yp1, yp2 = weights
         base = (c * levels + k) * tall + PADR + 8 * g
         value = flat[pl.ds(pl.multiple_of(base, 8), 8), :]
-        beside = pltpu.roll(cols[c, pl.ds(8 * g, 8), :], 126 - 4 * k, 1)
         total = centre * value
+        total += ym2 * flat[pl.ds(base - 2, 8), :]
+        total += ym1 * flat[pl.ds(base - 1, 8), :]
+        total += yp1 * flat[pl.ds(base + 1, 8), :]
+        total += yp2 * flat[pl.ds(base + 2, 8), :]
         total += xm2 * pltpu.roll(jnp.where(lane >= 126, beside, value), 2, 1)
         total += xm1 * pltpu.roll(jnp.where(lane == 127, beside, value), 1, 1)
         total += xp1 * pltpu.roll(jnp.where(lane == 0, beside, value), 127, 1)
         total += xp2 * pltpu.roll(jnp.where(lane <= 1, beside, value), 126, 1)
-        total += ym2 * flat[pl.ds(base - 2, 8), :]
-        total += ym1 * flat[pl.ds(base - 1, 8), :]
-        total += yp1 * flat[pl.ds(base + 1, 8), :]
-        total += yp2 * flat[pl.ds(base + 2, 8), :]
         return total
 
     def first_step(part):
-        def level(k, acc):
-            acc = list(acc)
+        count = tracer_count + 1
+
+        def pack(acc, done, k):
             here = group == k
+            shift = (4 * k + 2) & 127
+            return tuple(jnp.where(here, pltpu.roll(v, shift, 1), a) for a, v in zip(acc, done))
+
+        def level(k, carry):
+            acc, done, sides = carry
+            acc = pack(acc, done, k - 1)
+            ahead = sides_of(part, k + 1, count)
+            done = []
             for n, g in enumerate(parts[part]):
-                weights = make_coefficients(k, g)
+                weights = make_coefficients(k, g, sides[n * count + tracer_count])
                 for w, weight in enumerate(weights):
                     coef[k, w, pl.ds(8 * g, 8), :] = weight
                 for c in range(tracer_count):
-                    value = apply(first_flat, k, g, c, weights)
+                    value = apply(first_flat, k, g, c, weights, sides[n * count + c])
                     second[c * levels + k, pl.ds(PADR + 8 * g, 8), :] = value
-                    i = n * tracer_count + c
-                    acc[i] = jnp.where(here, pltpu.roll(value, 4 * k + 2, 1), acc[i])
-            return tuple(acc)
+                    done.append(value)
+            return acc, tuple(done), ahead
 
         start = (blank,) * (tracer_count * len(parts[part]))
-        return lax.fori_loop(0, levels, level, start, unroll=2)
+        acc, done, _ = lax.fori_loop(
+            0, levels, level, (start, start, sides_of(part, 0, count)), unroll=2
+        )
+        return pack(acc, done, levels - 1)
 
     def second_step(part):
-        def level(k, carry):
-            for g in parts[part]:
+        def level(k, sides):
+            ahead = sides_of(part, k + 1, tracer_count)
+            for n, g in enumerate(parts[part]):
                 weights = [coef[k, w, pl.ds(8 * g, 8), :] for w in range(9)]
                 for c in range(tracer_count):
-                    final[c * levels + k, pl.ds(8 * g, 8), :] = apply(second_flat, k, g, c, weights)
-            return carry
-
-        lax.fori_loop(0, levels, level, 0, unroll=2)
+                    final[c * levels + k, pl.ds(8 * g, 8), :] = apply(
+                        second_flat, k, g, c, weights, sides[n * tracer_count + c]
+                    )
+            return ahead
+
+        lax.fori_loop(0, levels, level, sides_of(part, 0, tracer_count), unroll=2)
 
     fill_rows(first_flat, 0)
     pl.semaphore_wait(barrier, n_dev - 1)
@@ -360,6 +381,7 @@
         pick[pl.ds(start, 128), :] = jnp.where(place == wanted, 1.0, 0.0).astype(jnp.bfloat16)
         return carry
 
+    taken[...] = jnp.zeros_like(taken)
     lax.fori_loop(0, rows, mark, 0)
 
     wait_columns(0, 0)
@@ -379,27 +401,34 @@
 
     flat = final.reshape(planes * rows, 128)
 
-    def take(low, high):
-        for r in range(low, high):
-            value = flat[pl.ds(r, planes, stride=rows), :]
-            upper_half = value.astype(jnp.bfloat16)
-            rest = (value - upper_half.astype(jnp.float32)).astype(jnp.bfloat16)
-            halves[pl.ds(0, planes), pl.ds(r * 128, 128)] = upper_half
-            halves[pl.ds(planes, planes), pl.ds(r * 128, 128)] = rest
-        span = pl.ds(low * 128, (high - low) * 128)
-        return jnp.dot(halves[:, span], pick[span, :], preferred_element_type=jnp.float32)
+    def take(part):
+        half = rows // 8
+
+        def four_rows(i, carry):
+            start = 4 * (half // 2 + i) if part == 0 else 4 * jnp.where(i < half // 2, i, i + half)
+            for j in range(4):
+                value = flat[pl.ds(start + j, planes, stride=rows), :]
+                high = value.astype(jnp.bfloat16)
+                rest = (value - high.astype(jnp.float32)).astype(jnp.bfloat16)
+                halves[pl.ds(0, planes), pl.ds(j * 128, 128)] = high
+                halves[pl.ds(planes, planes), pl.ds(j * 128, 128)] = rest
+            chosen = pick[pl.ds(pl.multiple_of(start * 128, 512), 512), :]
+            taken[...] += jnp.dot(halves[...], chosen, preferred_element_type=jnp.float32)
+            return carry
+
+        lax.fori_loop(0, half, four_rows, 0)
 
     wait_columns(1, 0)
     place_columns(1, 0)
     second_step(0)
-    taken[...] = take(8, rows - 8)
+    take(0)
     wait_rows(1)
     place_rows(second_flat, 1)
     wait_columns(1, 1)
     place_columns(1, 1)
     second_step(1)
-    both = taken[...] + take(0, 8) + take(rows - 8, rows)
-    outbox[...] = jnp.transpose(both[:planes] + both[planes:]) + tally
+    take(1)
+    outbox[...] = jnp.transpose(taken[pl.ds(0, planes), :] + taken[pl.ds(planes, planes), :]) + tally
 
     def box_copy(j):
         other = lax.rem(me + j, n_dev)
@@ -480,7 +509,7 @@
             *[pltpu.VMEM((2, 2, col_size, columns), f32)] * 4,
             *[pltpu.VMEM((2, row_size, columns), f32)] * 4,
             pltpu.VMEM((rows * columns, n_dev * BOX), jnp.bfloat16),
-            pltpu.VMEM((2 * planes, rows * columns), jnp.bfloat16),
+            pltpu.VMEM((2 * planes, 4 * columns), jnp.bfloat16),
             pltpu.VMEM((2 * planes, n_dev * BOX), f32),
             pltpu.VMEM((n_dev * BOX, planes), f32),
             pltpu.VMEM((n_dev * BOX, planes), f32),

time: 41.3 us -> 39.7 us (0.961)
  Pallas kernels: 38 us -> 36.5 us
    pallas_call x1, Pallas kernels: 38 us -> 36.5 us  [local(): pl.pallas_call(functools.partial(kernel, (tracer_count, levels, rows, n_l...]
where the time goes in v5:
time: 39.7 us; the launch traced here: 39.6 us
  Pallas kernels  36.5 us (92%)
  local copies, waits for them, and re-layouts  2.46 us (6%)
  between operations  0.64 us (2%)
    pallas_call x1, Pallas kernels, local(): pl.pallas_call(functools.partial(kernel, (tracer_count, levels, rows, n_l...  36.5 us
    unnamed x3, local copies, waits for them, and re-layouts  2.46 us

profile of v5, /device:TPU:0, one launch (start us, length us, event | category | flops | bytes accessed | tf_op | source)
XLA Modules:
  0.0 39.6 jit_solution(14377518779256436191)
XLA Ops:
  0.6 36.5 %shard_map.94 = (f32[128,32,128]{2,1,0:T(8,128)S(1)}, f32[128,128]{1,0:T(8,128)S(1)}, s32[1,32]{1,0:T(1,128)S(1)}) custom-call(f32[32,128]{1,0:T(8,128)} %area_h.1, s32[1,64]{1,0:T(1,128)} %bitcast.8, s32[1,64]{1,0:T(1,128)} %bitcast.9, s32[32,32,128]{2,1,0:T(8,128)} %mask_h.1, f32[32,32,128]{2,1,0:T(8,128)} %east_h.1, f32[32,32,128]{2,1,0:T(8,128)} %north_h.1, ...), custom_call_target="tpu_custom_call" | custom-call | flops 17825792 | bytes 8388608 | tf_op jit(solution)/shard_map/pallas_call | solution.py:487
  37.1 1.3 %copy.13 = f32[4,32,32,128]{3,2,1,0:T(8,128)} copy(f32[4,32,32,128]{3,2,1,0:T(8,128)S(1)} %bitcast.5) | data formatting | bytes 4194304
  38.4 0.5 %copy.15 = s32[32]{0:T(128)} copy(s32[32]{0:T(128)S(1)} %bitcast.6) | data formatting | bytes 256
  39.0 0.6 %copy.14 = f32[128,128]{1,0:T(8,128)} copy(f32[128,128]{1,0:T(8,128)S(1)} %get-tuple-element.10) | data formatting | bytes 131072

commit v6 on v5

--- a/solution.py
+++ b/solution.py
@@ -138,21 +138,21 @@
 
         @pl.when(top)
         def _():
-            ahead = lax.broadcasted_iota(jnp.int32, (128, 128), 0)
-            across = lax.broadcasted_iota(jnp.int32, (128, 128), 1)
-            turn = (ahead + across == 127).astype(jnp.float32)
-
-            def reverse(i, carry):
-                at = pl.ds(pl.multiple_of(i * levels, levels), levels)
+            ahead = lax.rem(lax.broadcasted_iota(jnp.int32, (256, 128), 0), 128)
+            across = lax.broadcasted_iota(jnp.int32, (256, 128), 1)
+            turn = jnp.where(ahead + across == 127, 1.0, 0.0).astype(jnp.bfloat16)
+
+            def reverse(at):
+                value = send_n[step, at, :]
+                high = value.astype(jnp.bfloat16)
+                rest = (value - high.astype(jnp.float32)).astype(jnp.bfloat16)
                 send_n[step, at, :] = jnp.dot(
-                    send_n[step, at, :],
-                    turn,
-                    precision=lax.Precision.HIGHEST,
-                    preferred_element_type=jnp.float32,
+                    jnp.concatenate([high, rest], axis=1), turn, preferred_element_type=jnp.float32
                 )
-                return carry
-
-            lax.fori_loop(0, 2 * tracer_count + (1 if step == 0 else 0), reverse, 0)
+
+            reverse(pl.ds(0, 2 * planes))
+            if step == 0:
+                reverse(pl.ds(2 * planes, levels))
 
         send_s[step, pl.ds(0, planes), :] = row(0)
         send_s[step, pl.ds(planes, planes), :] = row(1)
@@ -328,7 +328,7 @@
 
         start = (blank,) * (tracer_count * len(parts[part]))
         acc, done, _ = lax.fori_loop(
-            0, levels, level, (start, start, sides_of(part, 0, count)), unroll=2
+            0, levels, level, (start, start, sides_of(part, 0, count)), unroll=4
         )
         return pack(acc, done, levels - 1)
 
@@ -343,7 +343,7 @@
                     )
             return ahead
 
-        lax.fori_loop(0, levels, level, sides_of(part, 0, tracer_count), unroll=2)
+        lax.fori_loop(0, levels, level, sides_of(part, 0, tracer_count), unroll=4)
 
     fill_rows(first_flat, 0)
     pl.semaphore_wait(barrier, n_dev - 1)
@@ -430,39 +430,34 @@
     take(1)
     outbox[...] = jnp.transpose(taken[pl.ds(0, planes), :] + taken[pl.ds(planes, planes), :]) + tally
 
-    def box_copy(j):
-        other = lax.rem(me + j, n_dev)
-        return pltpu.make_async_remote_copy(
+    own = pl.ds(pl.multiple_of(me * BOX, BOX), BOX)
+
+    def after_me(j):
+        return jnp.where(me + j >= n_dev, me + j - n_dev, me + j)
+
+    def box_start(j, carry):
+        other = after_me(j)
+        pltpu.make_async_remote_copy(
             src_ref=outbox.at[pl.ds(pl.multiple_of(other * BOX, BOX), BOX)],
-            dst_ref=inbox.at[pl.ds(pl.multiple_of(me * BOX, BOX), BOX)],
-            send_sem=box_send.at[other],
-            recv_sem=box_recv.at[me],
-            device_id=(other // n_lon, lax.rem(other, n_lon)),
+            dst_ref=inbox.at[own],
+            send_sem=box_send.at[0],
+            recv_sem=box_recv.at[0],
+            device_id=(lax.div(other, n_lon), lax.rem(other, n_lon)),
             device_id_type=MESH,
-        )
-
-    def box_start(j, carry):
-        box_copy(j).start()
+        ).start()
         return carry
 
-    def box_wait(j, carry):
-        other = lax.rem(me + j, n_dev)
-        at = pl.ds(pl.multiple_of(other * BOX, BOX), BOX)
-        copy = pltpu.make_async_remote_copy(
-            src_ref=outbox.at[at],
-            dst_ref=inbox.at[at],
-            send_sem=box_send.at[other],
-            recv_sem=box_recv.at[other],
-            device_id=(other // n_lon, lax.rem(other, n_lon)),
-            device_id_type=MESH,
-        )
-        copy.wait()
-        return carry
-
     lax.fori_loop(1, n_dev, box_start, 0)
-    own = pl.ds(pl.multiple_of(me * BOX, BOX), BOX)
+    others = pl.ds(0, (n_dev - 1) * BOX)
+    pltpu.make_async_remote_copy(
+        src_ref=outbox.at[others],
+        dst_ref=inbox.at[others],
+        send_sem=box_send.at[0],
+        recv_sem=box_recv.at[0],
+        device_id=(lat, right),
+        device_id_type=MESH,
+    ).wait()
     inbox[own, :] = outbox[own, :]
-    lax.fori_loop(1, n_dev, box_wait, 0)
     for i in range(CAP):
         arrivals[pl.ds(i, n_dev, stride=CAP), :] = inbox[pl.ds(i, n_dev, stride=BOX), :]
     told = inbox[pl.ds(CAP, n_dev, stride=BOX), :][:, :n_dev]
@@ -516,8 +511,8 @@
             pltpu.SemaphoreType.DMA((7,)),
             pltpu.SemaphoreType.DMA((2, 6)),
             pltpu.SemaphoreType.DMA((2, 6)),
-            pltpu.SemaphoreType.DMA((n_dev,)),
-            pltpu.SemaphoreType.DMA((n_dev,)),
+            pltpu.SemaphoreType.DMA((1,)),
+            pltpu.SemaphoreType.DMA((1,)),
         ],
         compiler_params=pltpu.CompilerParams(
             collective_id=0, has_side_effects=True, vmem_limit_bytes=56 * 1024 * 1024

time: 39.7 us -> 37.2 us (0.937)
  Pallas kernels: 36.5 us -> 33.9 us
    pallas_call x1, Pallas kernels: 36.5 us -> 33.9 us  [local(): pl.pallas_call(functools.partial(kernel, (tracer_count, levels, rows, n_l...]
where the time goes in v6:
time: 37.2 us; the launch traced here: 37 us
  Pallas kernels  33.9 us (91%)
  local copies, waits for them, and re-layouts  2.46 us (7%)
  between operations  0.64 us (2%)
    pallas_call x1, Pallas kernels, local(): pl.pallas_call(functools.partial(kernel, (tracer_count, levels, rows, n_l...  33.9 us
    unnamed x3, local copies, waits for them, and re-layouts  2.46 us

profile of v6, /device:TPU:0, one launch (start us, length us, event | category | flops | bytes accessed | tf_op | source)
XLA Modules:
  0.0 37.0 jit_solution(15343016458729953864)
XLA Ops:
  0.6 33.9 %shard_map.94 = (f32[128,32,128]{2,1,0:T(8,128)S(1)}, f32[128,128]{1,0:T(8,128)S(1)}, s32[1,32]{1,0:T(1,128)S(1)}) custom-call(f32[32,128]{1,0:T(8,128)} %area_h.1, s32[1,64]{1,0:T(1,128)} %bitcast.8, s32[1,64]{1,0:T(1,128)} %bitcast.9, s32[32,32,128]{2,1,0:T(8,128)} %mask_h.1, f32[32,32,128]{2,1,0:T(8,128)} %east_h.1, f32[32,32,128]{2,1,0:T(8,128)} %north_h.1, ...), custom_call_target="tpu_custom_call" | custom-call | flops 17825792 | bytes 8388608 | tf_op jit(solution)/shard_map/pallas_call | solution.py:482
  34.6 1.3 %copy.13 = f32[4,32,32,128]{3,2,1,0:T(8,128)} copy(f32[4,32,32,128]{3,2,1,0:T(8,128)S(1)} %bitcast.5) | data formatting | bytes 4194304
  35.9 0.5 %copy.15 = s32[32]{0:T(128)} copy(s32[32]{0:T(128)S(1)} %bitcast.6) | data formatting | bytes 256
  36.4 0.6 %copy.14 = f32[128,128]{1,0:T(8,128)} copy(f32[128,128]{1,0:T(8,128)S(1)} %get-tuple-element.10) | data formatting | bytes 131072

commit v7 on v6

--- a/solution.py
+++ b/solution.py
@@ -45,10 +45,16 @@
 
     barrier = pltpu.get_barrier_semaphore()
 
+    def after_me(j):
+        return jnp.where(me + j >= n_dev, me + j - n_dev, me + j)
+
     def greet(j, carry):
-        other = lax.rem(me + j, n_dev)
+        other = after_me(j)
         pl.semaphore_signal(
-            barrier, inc=1, device_id=(other // n_lon, lax.rem(other, n_lon)), device_id_type=MESH
+            barrier,
+            inc=1,
+            device_id=(lax.div(other, n_lon), lax.rem(other, n_lon)),
+            device_id_type=MESH,
         )
         return carry
 
@@ -432,14 +438,11 @@
 
     own = pl.ds(pl.multiple_of(me * BOX, BOX), BOX)
 
-    def after_me(j):
-        return jnp.where(me + j >= n_dev, me + j - n_dev, me + j)
-
     def box_start(j, carry):
         other = after_me(j)
         pltpu.make_async_remote_copy(
-            src_ref=outbox.at[pl.ds(pl.multiple_of(other * BOX, BOX), BOX)],
-            dst_ref=inbox.at[own],
+            src_ref=outbox.at[pl.ds(pl.multiple_of(other * BOX, BOX), CAP + 1)],
+            dst_ref=inbox.at[pl.ds(pl.multiple_of(me * BOX, BOX), CAP + 1)],
             send_sem=box_send.at[0],
             recv_sem=box_recv.at[0],
             device_id=(lax.div(other, n_lon), lax.rem(other, n_lon)),
@@ -448,7 +451,7 @@
         return carry
 
     lax.fori_loop(1, n_dev, box_start, 0)
-    others = pl.ds(0, (n_dev - 1) * BOX)
+    others = pl.ds(0, (n_dev - 1) * (CAP + 1))
     pltpu.make_async_remote_copy(
         src_ref=outbox.at[others],
         dst_ref=inbox.at[others],

time: 37.2 us -> 36.9 us (level)
  no operation moved by 1% of the time
where the time goes in v7:
time: 36.9 us; the launch traced here: 36.7 us
  Pallas kernels  33.6 us (91%)
  local copies, waits for them, and re-layouts  2.46 us (7%)
  between operations  0.64 us (2%)
    pallas_call x1, Pallas kernels, local(): pl.pallas_call(functools.partial(kernel, (tracer_count, levels, rows, n_l...  33.6 us
    unnamed x3, local copies, waits for them, and re-layouts  2.46 us

profile of v7, /device:TPU:0, one launch (start us, length us, event | category | flops | bytes accessed | tf_op | source)
XLA Modules:
  0.0 36.7 jit_solution(8887610648313517269)
XLA Ops:
  0.6 33.6 %shard_map.94 = (f32[128,32,128]{2,1,0:T(8,128)S(1)}, f32[128,128]{1,0:T(8,128)S(1)}, s32[1,32]{1,0:T(1,128)S(1)}) custom-call(f32[32,128]{1,0:T(8,128)} %area_h.1, s32[1,64]{1,0:T(1,128)} %bitcast.8, s32[1,64]{1,0:T(1,128)} %bitcast.9, s32[32,32,128]{2,1,0:T(8,128)} %mask_h.1, f32[32,32,128]{2,1,0:T(8,128)} %east_h.1, f32[32,32,128]{2,1,0:T(8,128)} %north_h.1, ...), custom_call_target="tpu_custom_call" | custom-call | flops 17825792 | bytes 8388608 | tf_op jit(solution)/shard_map/pallas_call | solution.py:485
  34.3 1.3 %copy.13 = f32[4,32,32,128]{3,2,1,0:T(8,128)} copy(f32[4,32,32,128]{3,2,1,0:T(8,128)S(1)} %bitcast.5) | data formatting | bytes 4194304
  35.6 0.5 %copy.15 = s32[32]{0:T(128)} copy(s32[32]{0:T(128)S(1)} %bitcast.6) | data formatting | bytes 256
  36.1 0.6 %copy.14 = f32[128,128]{1,0:T(8,128)} copy(f32[128,128]{1,0:T(8,128)S(1)} %get-tuple-element.10) | data formatting | bytes 131072
